TPU v7x, 256 devices: a whole 4x4x8 slice. The times are simulated.
256 devices in a mesh: pipe: 16 (over y_lo, x, core), expert: 16 (over y_hi, z).
Axes of the slice: x: 4, y: 4 (y_hi: 2, y_lo: 2; y = y_hi * 2 + y_lo), z: 8, core: 2. Of those that a mesh axis runs over, the one named last changes fastest.
Arguments:
- held_fwd: bfloat16 [16, 1024, 3584], P('pipe', 'expert'), may hold values from -6 to 6
- ids_fwd: int32 [16, 1024], P('pipe'), may hold values from 0 to 3, as said below
- probs_fwd: bfloat16 [16, 1024], P('pipe'), may hold values from 0.19921875 to 1
- saved_in: bfloat16 [16, 1024, 3584], P('pipe', 'expert'), may hold values from -6 to 6
- held_grad: bfloat16 [16, 1024, 3584], P('pipe', 'expert'), may hold values from -6 to 6
- ids_bwd: int32 [16, 1024], P('pipe'), may hold values from 0 to 3, as said below
- probs_bwd: bfloat16 [16, 1024], P('pipe'), may hold values from 0.19921875 to 1
- w_gate: bfloat16 [16, 3584, 6144], P('pipe', None, 'expert'), may hold values from -0.09375 to 0.09375
- w_up: bfloat16 [16, 3584, 6144], P('pipe', None, 'expert'), may hold values from -0.09375 to 0.09375
- w_down: bfloat16 [16, 6144, 3584], P('pipe', 'expert'), may hold values from -0.15625 to 0.15625
Outputs:
- fwd_out: bfloat16 [16, 1024, 3584], P('pipe', 'expert')
- grad_out: bfloat16 [16, 1024, 3584], P('pipe', 'expert')
Inputs may be any that keep to these rules, and one draw needn't show every extreme that they name: `ids_fwd`: in every section one expert takes exactly 20 of the 64 rows of each device, 320 rows in all; no expert takes more than 20 of the rows of one device. `ids_bwd`: in every section one expert takes exactly 20 of the 64 rows of each device, 320 rows in all; no expert takes more than 20 of the rows of one device.
All inputs are finite; a program needn't handle non-finite values.
Results may differ from a plain program's by a relative error of at most 0.004.
Values may be sent and summed in bfloat16 or wider, within the bound.
A program may use at most 128 MiB of HBM per device.

v0:
```python
import jax
import jax.numpy as jnp
from jax import lax
from jax.sharding import PartitionSpec as P

EXPERTS = 4
SLOT = 20


def passed_along(value, axis, by):
    devices = lax.axis_size(axis)
    return lax.ppermute(value, axis, [(i, (i + by) % devices) for i in range(devices)])


def chosen_rows(routing, expert, capacity):
    matches = routing == expert
    places = jnp.nonzero(matches, size=capacity, fill_value=0)[0].astype(jnp.int32)
    filled = jnp.arange(capacity, dtype=jnp.int32) < jnp.sum(matches.astype(jnp.int32))
    return (places, filled)


def expert_forward(row_block, row_scale, gate_cols, up_cols, down_rows):
    gate_pre = jnp.dot(row_block, gate_cols, preferred_element_type=jnp.float32)
    upward = jnp.dot(row_block, up_cols, preferred_element_type=jnp.float32)
    hidden = (gate_pre * jax.nn.sigmoid(gate_pre) * upward).astype(jnp.bfloat16)
    return jnp.dot(hidden, down_rows, preferred_element_type=jnp.float32) * row_scale[:, None]


def expert_backward(row_block, grad_block, row_scale, gate_cols, up_cols, down_rows):
    gate_pre = jnp.dot(row_block, gate_cols, preferred_element_type=jnp.float32)
    upward = jnp.dot(row_block, up_cols, preferred_element_type=jnp.float32)
    d_hidden = (
        jnp.dot(grad_block, down_rows.T, preferred_element_type=jnp.float32) * row_scale[:, None]
    )
    sigmoid_gate = jax.nn.sigmoid(gate_pre)
    d_gate = (d_hidden * upward * sigmoid_gate * (1.0 + gate_pre * (1.0 - sigmoid_gate))).astype(
        jnp.bfloat16
    )
    d_up = (d_hidden * gate_pre * sigmoid_gate).astype(jnp.bfloat16)
    result = jnp.dot(d_gate, gate_cols.T, preferred_element_type=jnp.float32)
    return result + jnp.dot(d_up, up_cols.T, preferred_element_type=jnp.float32)


def expert_slots(local_ids, local_probs, slot_total):
    place_list = []
    scale_list = []
    for expert in range(EXPERTS):
        places, filled = chosen_rows(local_ids, expert, slot_total)
        place_list.append(places)
        scale_list.append(jnp.where(filled, local_probs[places], jnp.zeros((), local_probs.dtype)))
    return (jnp.stack(place_list), jnp.stack(scale_list))


def source_places(routing_all, expert, slot_total, local_total):
    blocks = routing_all.reshape(-1, local_total)

    def one_block(block_ids):
        return chosen_rows(block_ids, expert, slot_total)

    places, filled = jax.vmap(one_block)(blocks)
    offsets = (jnp.arange(blocks.shape[0], dtype=jnp.int32) * local_total)[:, None]
    return ((places + offsets).reshape(-1), filled.reshape(-1))


def combine_slots(returned, places_all, local_total):
    feature_width = returned.shape[2]
    grouped = jnp.sum(
        returned.reshape(EXPERTS, -1, returned.shape[1], feature_width), axis=1, dtype=jnp.float32
    )
    empty_rows = jnp.zeros((local_total, feature_width), jnp.float32)
    return empty_rows.at[places_all.reshape(-1)].add(grouped.reshape(-1, feature_width))


def on_device(
    held_fwd, ids_fwd, probs_fwd, saved_in, held_grad, ids_bwd, probs_bwd, w_gate, w_up, w_down
):
    devices = lax.axis_size("expert")
    group_size = devices // EXPERTS
    position = lax.axis_index("expert")
    my_expert = position // group_size
    gate_cols = w_gate[0]
    up_cols = w_up[0]
    down_rows = w_down[0]
    rows_fwd = passed_along(held_fwd[0], "pipe", 1)
    grads_in = passed_along(held_grad[0], "pipe", -1)
    saved_rows = saved_in[0]
    local_total = rows_fwd.shape[0]
    feature_width = rows_fwd.shape[1]
    slot_total = SLOT
    first_row = position * local_total
    local_fwd = lax.dynamic_slice_in_dim(ids_fwd[0], first_row, local_total)
    prob_fwd = lax.dynamic_slice_in_dim(probs_fwd[0], first_row, local_total)
    places_all, scales_all = expert_slots(local_fwd, prob_fwd, slot_total)
    local_bwd = lax.dynamic_slice_in_dim(ids_bwd[0], first_row, local_total)
    prob_bwd = lax.dynamic_slice_in_dim(probs_bwd[0], first_row, local_total)
    places_back, scales_back = expert_slots(local_bwd, prob_bwd, slot_total)
    gathered = lax.all_gather(rows_fwd, "expert", axis=0, tiled=True)
    picked, filled = source_places(ids_fwd[0], my_expert, slot_total, local_total)
    row_scale = jnp.where(filled, probs_fwd[0][picked].astype(jnp.float32), 0.0)
    partial_value = expert_forward(gathered[picked], row_scale, gate_cols, up_cols, down_rows)
    back_rows = partial_value.astype(jnp.bfloat16).reshape(devices, slot_total, feature_width)
    returned = lax.all_to_all(back_rows, "expert", split_axis=0, concat_axis=0, tiled=True)
    summed = combine_slots(returned, places_all, local_total)
    saved_all, grads_all = (
        lax.all_gather(saved_rows, "expert", axis=0, tiled=True),
        lax.all_gather(grads_in, "expert", axis=0, tiled=True),
    )
    picked_back, filled_back = source_places(ids_bwd[0], my_expert, slot_total, local_total)
    scale_back = jnp.where(filled_back, probs_bwd[0][picked_back].astype(jnp.float32), 0.0)
    partial_back = expert_backward(
        saved_all[picked_back], grads_all[picked_back], scale_back, gate_cols, up_cols, down_rows
    )
    back_grads = partial_back.astype(jnp.bfloat16).reshape(devices, slot_total, feature_width)
    returned_back = lax.all_to_all(back_grads, "expert", split_axis=0, concat_axis=0, tiled=True)
    summed_back = combine_slots(returned_back, places_back, local_total)
    fwd_rows = (rows_fwd + summed).astype(jnp.bfloat16)
    grad_rows = (grads_in + summed_back).astype(jnp.bfloat16)
    return (fwd_rows[None], grad_rows[None])


def solution(mesh):
    return jax.shard_map(
        on_device,
        mesh=mesh,
        in_specs=(
            P("pipe", "expert", None),
            P("pipe", None),
            P("pipe", None),
            P("pipe", "expert", None),
            P("pipe", "expert", None),
            P("pipe", None),
            P("pipe", None),
            P("pipe", None, "expert"),
            P("pipe", None, "expert"),
            P("pipe", "expert", None),
        ),
        out_specs=(P("pipe", "expert", None), P("pipe", "expert", None)),
        check_vma=False,
    )
```

profile of v0, /device:TPU:38, one launch (start us, length us, event | category | flops | bytes accessed | tf_op | source)
XLA Modules:
  0.0 525.6 jit_solution(459751190031298476)
XLA Ops:
  8.3 6.3 %collective-permute-done.1 = bf16[64,3584]{1,0:T(8,128)(2,1)S(1)} collective-permute-done((bf16[64,3584]{1,0:T(8,128)(2,1)}, bf16[64,3584]{1,0:T(8,128)(2,1)S(1)}, u32[]{:S(2)}, u32[]{:S(2)}) %collective-permute-start.1) | collective-permute-done | bytes 458784 | tf_op jit(solution)/shard_map/ppermute | solution.py:12
  15.5 3.6 collective-permute-start
  19.1 4.7 collective-permute-done
  25.1 1.4 fusion.108
  26.9 0.9 compare_select_fusion.1
  27.8 1.3 copy.53
  30.4 1.3 copy.62
  32.2 7.6 %scatter_custom_fusion.10 = s32[320]{0:T(512)S(1)} fusion(s32[1024]{0:T(1024)S(1)} %reshape.1353, s32[1024]{0:T(1024)S(1)} %broadcast.1072, s32[]{:T(128)} %constant.206.clone.1), kind=kCustom, calls=%fused_computation.151 | custom fusion | flops 1024 | bytes 1284
  40.5 7.8 %scatter_custom_fusion.11 = s32[320]{0:T(512)S(1)} fusion(s32[1024]{0:T(1024)S(1)} %reshape.1359, s32[1024]{0:T(1024)S(1)} %broadcast.1072, s32[]{:T(128)} %constant.206.clone.1), kind=kCustom, calls=%fused_computation.149 | custom fusion | flops 1024 | bytes 1284
  49.7 2.5 gather_fusion.3
  52.2 85.1 %all-gather.9.cloned.1.call-done = bf16[1,1024,3584]{2,1,0:T(8,128)(2,1)} async-done(((bf16[1,64,3584]{2,1,0:T(8,128)(2,1)}), bf16[1,1024,3584]{2,1,0:T(8,128)(2,1)}) %all-gather.9.cloned.1.call-update) | async-done | bytes 7340048 | tf_op jit(solution)/shard_map/all_gather | solution.py:105
  137.4 11.5 %gather_fusion.4 = bf16[320,3584]{1,0:T(8,128)(2,1)} fusion(bf16[1024,3584]{1,0:T(8,128)(2,1)} %bitcast.85, s32[1024]{0:T(1024)S(1)} %pad_clamp_fusion), kind=kCustom, calls=%fused_computation.4 | custom fusion | bytes 4588800 | tf_op jit(solution)/shard_map/gather | solution.py:111
  148.8 4.0 fusion.12
  152.8 110.1 %all-gather.7.cloned.1.call-done = bf16[1024,3584]{1,0:T(8,128)(2,1)} async-done(((bf16[64,3584]{1,0:T(8,128)(2,1)}), bf16[1024,3584]{1,0:T(8,128)(2,1)}) %all-gather.7.cloned.1.call-update) | async-done | bytes 7340048 | tf_op jit(solution)/shard_map/all_gather | solution.py:106
  262.9 11.7 %gather_fusion.2 = bf16[320,3584]{1,0:T(8,128)(2,1)} fusion(bf16[1024,3584]{1,0:T(8,128)(2,1)} %all-gather.7.cloned.1.call-done, s32[1024]{0:T(1024)S(1)} %pad_clamp_fusion), kind=kCustom, calls=%fused_computation.2 | custom fusion | bytes 4588800 | tf_op jit(solution)/shard_map/gather | solution.py:111
  274.6 4.8 fusion.25
  279.4 7.5 %fusion.10 = f32[320,3584]{1,0:T(8,128)} fusion(bf16[1,3584,384]{2,1,0:T(8,128)(2,1)} %param.17, f32[320,384]{1,0:T(8,128)} %fusion.25, bf16[320,3584]{1,0:T(8,128)(2,1)} %gather_fusion.4, bf16[1,3584,384]{2,1,0:T(8,128)(2,1)S(1)} %copy-done, f32[320,384]{1,0:T(8,128)S(1)} %fusion.12), kind=kOutput, calls=%fused_computation.31 | convolution fusion | flops 1762836480 | bytes 13369344 | tf_op jit(solution)/shard_map/dot_general | solution.py:40
  286.9 5.3 %fusion.1 = bf16[320,3584]{1,0:T(8,128)(2,1)} fusion(f32[320,3584]{1,0:T(8,128)} %fusion.10, bf16[1,3584,384]{2,1,0:T(8,128)(2,1)S(1)} %copy-done, f32[320,384]{1,0:T(8,128)} %fusion.25, f32[320,384]{1,0:T(8,128)S(1)} %fusion.12), kind=kOutput, calls=%fused_computation.22 | convolution fusion | flops 883834880 | bytes 10616832 | tf_op jit(solution)/shard_map/dot_general | solution.py:41
  292.1 4.1 reshape.1209
  296.3 6.4 %all-to-all-start.1 = ((bf16[16,20,3584]{2,1,0:T(8,128)(2,1)}), bf16[16,20,3584]{2,1,0:T(8,128)(2,1)}, u32[]{:S(2)}, u32[]{:S(2)}) async-start(bf16[16,20,3584]{2,1,0:T(8,128)(2,1)} %reshape.1209), calls=%async_computation.1 | async-start | bytes 5505024 | tf_op jit(solution)/shard_map/all_to_all | solution.py:114
  302.8 2.5 gather_fusion.1
  306.0 109.4 %all-gather.5.cloned.1.call-done = bf16[1024,3584]{1,0:T(8,128)(2,1)} async-done(((bf16[64,3584]{1,0:T(8,128)(2,1)}), bf16[1024,3584]{1,0:T(8,128)(2,1)}) %all-gather.5.cloned.1.call-update) | async-done | bytes 7340048 | tf_op jit(solution)/shard_map/all_gather | solution.py:97
  415.4 11.5 %gather_fusion = bf16[320,3584]{1,0:T(8,128)(2,1)} fusion(bf16[1024,3584]{1,0:T(8,128)(2,1)} %all-gather.5.cloned.1.call-done, s32[1024]{0:T(1024)S(1)} %pad_clamp_fusion.1), kind=kCustom, calls=%fused_computation | custom fusion | bytes 4588800 | tf_op jit(solution)/shard_map/gather | solution.py:100
  426.8 3.0 fusion.8
  429.8 5.9 %fusion = bf16[320,3584]{1,0:T(8,128)(2,1)S(1)} fusion(bf16[1,384,3584]{2,1,0:T(8,128)(2,1)} %param.19, f32[320]{0:T(512)S(1)} %convert_select_fusion.1, f32[320,384]{1,0:T(8,128)S(1)} %fusion.8, bf16[320,3584]{1,0:T(8,128)(2,1)} %gather_fusion, bf16[1,3584,384]{2,1,0:T(8,128)(2,1)} %param.17), kind=kOutput, calls=%fused_computation.21 | convolution fusion | flops 1764638720 | bytes 10585344 | tf_op jit(solution)/shard_map/dot_general | solution.py:26
  435.8 2.2 reshape.1202
  438.0 7.5 %all-to-all-start = ((bf16[16,20,3584]{2,1,0:T(8,128)(2,1)}), bf16[16,20,3584]{2,1,0:T(8,128)(2,1)}, u32[]{:S(2)}, u32[]{:S(2)}) async-start(bf16[16,20,3584]{2,1,0:T(8,128)(2,1)} %reshape.1202), calls=%async_computation | async-start | bytes 5505024 | tf_op jit(solution)/shard_map/all_to_all | solution.py:102
  445.9 1.0 scatter_custom_fusion.7
  447.4 1.0 scatter_custom_fusion.8
  448.9 1.0 scatter_custom_fusion.6
  450.4 1.0 scatter_custom_fusion.5
  452.3 1.3 compare_select_fusion.34
  453.6 1.2 compare_select_fusion.36
  455.9 1.0 scatter_custom_fusion.2
  457.4 1.0 scatter_custom_fusion.3
  458.9 1.0 scatter_custom_fusion.1
  460.4 1.0 scatter_custom_fusion
  462.3 1.3 compare_select_fusion.38
  463.6 1.2 compare_select_fusion.40
  465.0 1.0 convert_element_type.235
  466.0 2.4 convert_reduce_fusion
  468.4 1.2 reshape.1349
  469.6 3.1 scatter_fusion.1
  473.5 34.6 %all-to-all-done = bf16[16,20,3584]{2,1,0:T(8,128)(2,1)} async-done(((bf16[16,20,3584]{2,1,0:T(8,128)(2,1)}), bf16[16,20,3584]{2,1,0:T(8,128)(2,1)}, u32[]{:S(2)}, u32[]{:S(2)}) %all-to-all-start) | async-done | bytes 2293792 | tf_op jit(solution)/shard_map/all_to_all | solution.py:102
  508.1 2.4 convert_reduce_fusion.1
  510.5 1.1 reshape.1309
  511.6 5.0 scatter_fusion
  516.7 2.0 convert_bitcast_fusion.1
  (121 shorter events, 15.7 us)
Async XLA Ops:
  7.2 272.2 %copy-start = (bf16[1,3584,384]{2,1,0:T(8,128)(2,1)S(1)}, bf16[1,3584,384]{2,1,0:T(8,128)(2,1)}, u32[]{:S(2)}) copy-start(bf16[1,3584,384]{2,1,0:T(8,128)(2,1)} %param.18) | copy-start | bytes 8257540
  7.2 24.5 %copy-start.9 = (s32[2]{0:T(128)S(1)}, s32[2]{0:T(128)}, u32[]{:S(2)}) copy-start(s32[2]{0:T(128)} %constant.228) | copy-start | bytes 28
  7.2 130.2 %all-gather.9.cloned.1.call-start = ((), (), s32[]{:S(2)}) async-start(), calls=%async_computation.4 | async-start | bytes 7798784 | tf_op jit(solution)/shard_map/all_gather | solution.py:105
  7.9 23.9 %copy-start.8 = (s32[2]{0:T(128)S(1)}, s32[2]{0:T(128)}, u32[]{:S(2)}) copy-start(s32[2]{0:T(128)} %constant.231) | copy-start | bytes 28
  7.9 255.0 %all-gather.7.cloned.1.call-start = ((), (), s32[]{:S(2)}) async-start(), calls=%async_computation.3 | async-start | bytes 7798784 | tf_op jit(solution)/shard_map/all_gather | solution.py:106
  8.0 6.7 %collective-permute-start.1 = (bf16[64,3584]{1,0:T(8,128)(2,1)}, bf16[64,3584]{1,0:T(8,128)(2,1)S(1)}, u32[]{:S(2)}, u32[]{:S(2)}) collective-permute-start(bf16[64,3584]{1,0:T(8,128)(2,1)} %bitcast.88), channel_id=1, source_target_pairs={{0,240},{16,0},{32,16},{48,32},{64,48},{80,64},{96,80},{112,96},{1... | collective-permute-start | bytes 1376264 | tf_op jit(solution)/shard_map/ppermute | solution.py:12
  14.6 0.8 copy-start.2
  15.4 34.2 %copy-start.6 = (bf16[1,1024]{1,0:T(2,128)(2,1)S(1)}, bf16[1,1024]{1,0:T(2,128)(2,1)}, u32[]{:S(2)}) copy-start(bf16[1,1024]{1,0:T(2,128)(2,1)} %param.16) | copy-start | bytes 6148
  15.4 399.9 %all-gather.5.cloned.1.call-start = ((), (), s32[]{:S(2)}) async-start(), calls=%async_computation.2 | async-start | bytes 7798784 | tf_op jit(solution)/shard_map/all_gather | solution.py:97
  15.5 8.3 %collective-permute-start = (bf16[64,3584]{1,0:T(8,128)(2,1)}, bf16[64,3584]{1,0:T(8,128)(2,1)S(1)}, u32[]{:S(2)}, u32[]{:S(2)}) collective-permute-start(bf16[64,3584]{1,0:T(8,128)(2,1)} %bitcast.89), channel_id=1, source_target_pairs={{0,16},{16,32},{32,48},{48,64},{64,80},{80,96},{96,112},{112,128},... | collective-permute-start | bytes 1376264 | tf_op jit(solution)/shard_map/ppermute | solution.py:12
  23.8 0.8 copy-start.4
  296.3 6.4 %copy-start.7 = (bf16[1,1024]{1,0:T(2,128)(2,1)S(1)}, bf16[1,1024]{1,0:T(2,128)(2,1)}, u32[]{:S(2)}) copy-start(bf16[1,1024]{1,0:T(2,128)(2,1)} %param.12) | copy-start | bytes 6148
  296.3 141.8 %all-to-all-start.1 = ((bf16[16,20,3584]{2,1,0:T(8,128)(2,1)}), bf16[16,20,3584]{2,1,0:T(8,128)(2,1)}, u32[]{:S(2)}, u32[]{:S(2)}) async-start(bf16[16,20,3584]{2,1,0:T(8,128)(2,1)} %reshape.1209), calls=%async_computation.1 | async-start | bytes 5505024 | tf_op jit(solution)/shard_map/all_to_all | solution.py:114
  438.0 26.9 %copy-start.3 = (bf16[64,3584]{1,0:T(8,128)(2,1)S(1)}, bf16[64,3584]{1,0:T(8,128)(2,1)}, u32[]{:S(2)}) copy-start(bf16[64,3584]{1,0:T(8,128)(2,1)} %copy-done.2) | copy-start | bytes 1376260
  438.0 27.0 %copy-start.5 = (bf16[64,3584]{1,0:T(8,128)(2,1)S(1)}, bf16[64,3584]{1,0:T(8,128)(2,1)}, u32[]{:S(2)}) copy-start(bf16[64,3584]{1,0:T(8,128)(2,1)} %copy-done.4) | copy-start | bytes 1376260
  438.0 70.1 %all-to-all-start = ((bf16[16,20,3584]{2,1,0:T(8,128)(2,1)}), bf16[16,20,3584]{2,1,0:T(8,128)(2,1)}, u32[]{:S(2)}, u32[]{:S(2)}) async-start(bf16[16,20,3584]{2,1,0:T(8,128)(2,1)} %reshape.1202), calls=%async_computation | async-start | bytes 5505024 | tf_op jit(solution)/shard_map/all_to_all | solution.py:102
  511.6 7.0 %copy-start.1 = (bf16[1,3584,384]{2,1,0:T(8,128)(2,1)S(1)}, bf16[1,3584,384]{2,1,0:T(8,128)(2,1)}, u32[]{:S(2)}) copy-start(bf16[1,3584,384]{2,1,0:T(8,128)(2,1)} %param.18) | copy-start | bytes 8257540
Sparse Core Ops, SparseCore 0:
  10.6 126.6 all-gather.8
  140.5 122.3 all-gather.6
  266.1 149.2 all-gather.4
where the time goes:
time: 534 us; the launch traced here: 526 us
  waiting for transfers between devices  351 us (66%)
  local copies, waits for them, and re-layouts  56.3 us (11%)
  other arithmetic  55.5 us (10%)
  matrix products  30.4 us (6%)
  starting transfers between devices  17.9 us (3%)
  between operations  14.6 us (3%)
    all_gather x1, waiting for transfers between devices, on_device(): lax.all_gather(grads_in, 'expert', axis=0, tiled=True)  110 us
    all_gather x1, waiting for transfers between devices, on_device(): gathered = lax.all_gather(rows_fwd, 'expert', axis=0, tiled=True)  109 us
    all_gather x1, waiting for transfers between devices, on_device(): lax.all_gather(saved_rows, 'expert', axis=0, tiled=True)  85.1 us
    all_to_all x1, waiting for transfers between devices, on_device(): lax.all_to_all(back_rows, 'expert', split_axis=0, concat_axis=0, tiled=True)  34.6 us
    unnamed x8, other arithmetic  15.6 us
    gather x1, local copies, waits for them, and re-layouts, on_device(): grads_all[picked_back]  11.7 us
    gather x1, local copies, waits for them, and re-layouts, on_device(): gathered[picked]  11.5 us
    gather x1, local copies, waits for them, and re-layouts, on_device(): saved_all[picked_back]  11.5 us
  transfers between devices with their start and end apart: 7, of which 6 were waited for; matrix products, arithmetic and copies ran while one was open for 25% of the time, Pallas kernels for 0%

commit v1 on v0

v1 whole, which is shorter than its diff:
```python
import functools

import jax
import jax.numpy as jnp
from jax import lax
from jax.experimental import pallas as pl
from jax.experimental.pallas import tpu as pltpu
from jax.sharding import PartitionSpec as P

EXPERTS = 4
SLOT = 20
MESH = pl.DeviceIdType.MESH
F32 = jnp.float32
BF16 = jnp.bfloat16

D = 3584
HID = 384
TOK = 64
PAIR = 2 * SLOT
HALF = D // 2
WIDE = 512
CHUNKS = [slice(c, c + WIDE) for c in range(0, D, WIDE)]
STEPS = 6

OTHER, PASS = 8, 9
RECV, HOME, TRANSIT = 8, 17, 18


def pick(q, values):
    result = jnp.int32(values[3])
    for i in (2, 1, 0):
        result = jnp.where(q == i, jnp.int32(values[i]), result)
    return result


def mirrored(index):
    return 7 - index if index < 8 else index


def out_plan(right, k):
    plan = []
    for q in range(4):
        place = q if right else 3 - q
        active, src, dst = False, 0, 0
        if place < 2 and k < place + 3:
            active, src = True, place - k + 2
            dst = src
        elif place == 2:
            active = True
            src, dst = (OTHER, PASS) if k == 0 else (5 - k, 5 - k)
        elif place == 3 and k < 2:
            active, src, dst = True, OTHER + k, 1 - k
        if not right:
            src, dst = mirrored(src), mirrored(dst)
        plan.append((active, src, dst))
    return plan


def back_plan(left, k):
    plan = []
    for q in range(4):
        place = q if left else 3 - q
        active, src, dst, added = False, 0, 0, -1
        if 3 - place <= k <= 4:
            index = k - 3 + place
            active = True
            src = index if left else 7 - index
            slot = RECV + index if left else 16 - index
            dst = slot if place > 0 else TRANSIT - index
            added = slot if place < 3 else -1
        elif place == 3 and k == 5:
            active, src, dst = True, TRANSIT, HOME
        plan.append((active, src, dst, added))
    return plan


def kernel(
    held_fwd,
    held_grad,
    saved,
    slot_f_row,
    slot_f_col,
    prob_f,
    slot_b_row,
    slot_b_col,
    prob_b,
    w_gate_hbm,
    w_up_hbm,
    w_down_hbm,
    out_f,
    out_b,
    w_gate,
    w_up,
    w_down,
    x_rows,
    g_rows,
    ysend,
    yrecv,
    blk,
    ret,
    ysend_back,
    yrecv_back,
    packed,
    packed_g,
    act_a,
    act_b,
    fin,
    w_sem,
    shift_send,
    shift_recv,
    y_send_sem,
    y_recv_sem,
    out_send_sem,
    out_recv_sem,
    back_send_sem,
    back_recv_sem,
):
    pipe = lax.axis_index("pipe")
    position = lax.axis_index("expert")
    plane = position // 8
    z = position % 8
    half = z // 4
    q = z % 4
    right = (pipe, plane * 8 + (z + 1) % 8)
    left = (pipe, plane * 8 + (z + 7) % 8)
    across = (pipe, (1 - plane) * 8 + z)
    after = ((pipe + 1) % 16, position)
    before = ((pipe + 15) % 16, position)

    weight_copies = [
        pltpu.make_async_copy(w_gate_hbm, w_gate, w_sem.at[0]),
        pltpu.make_async_copy(w_up_hbm, w_up, w_sem.at[1]),
        pltpu.make_async_copy(w_down_hbm, w_down, w_sem.at[2]),
    ]
    for copy in weight_copies:
        copy.start()

    barrier = pltpu.get_barrier_semaphore()
    for device in (right, left, across, after, before):
        pl.semaphore_signal(barrier, inc=1, device_id=device, device_id_type=MESH)
    pl.semaphore_wait(barrier, 5)

    def remote(src, dst, send_sem, recv_sem, device):
        return pltpu.make_async_remote_copy(
            src_ref=src,
            dst_ref=dst,
            send_sem=send_sem,
            recv_sem=recv_sem,
            device_id=device,
            device_id_type=MESH,
        )

    shift_g = remote(held_grad, g_rows, shift_send.at[0], shift_recv.at[0], before)
    shift_x = remote(held_fwd, x_rows, shift_send.at[1], shift_recv.at[1], after)
    shift_g.start()
    shift_x.start()

    def grid(rows, cols):
        return (
            lax.broadcasted_iota(jnp.int32, (rows, cols), 0),
            lax.broadcasted_iota(jnp.int32, (rows, cols), 1),
        )

    def hot(mask):
        return jnp.where(mask, jnp.float32(1), jnp.float32(0)).astype(BF16)

    def dot(a, b):
        return jnp.dot(a, b, preferred_element_type=F32)

    def dot_t(a, b):
        return lax.dot_general(a, b, (((1,), (1,)), ((), ())), preferred_element_type=F32)

    sources = (saved, g_rows, x_rows)
    slot_rows = (slot_b_row, slot_b_row, slot_f_row)

    def y_copy(t):
        return remote(ysend.at[t], yrecv.at[t], y_send_sem.at[t], y_recv_sem.at[t], across)

    def send_across(t):
        row, _ = grid(PAIR, TOK)
        chosen = hot(row + (1 - plane) * PAIR == slot_rows[t][...])
        for c in CHUNKS:
            ysend[t, :, c] = dot(chosen, sources[t][:, c]).astype(BF16)
        y_copy(t).start()

    def build(t):
        y_copy(t).wait_recv()
        row, _ = grid(PAIR, TOK)
        to, frm = grid(PAIR, PAIR)
        for line, place in ((half, q + 2), (1 - half, OTHER)):
            own = hot((row < SLOT) & (row + (2 * plane + line) * SLOT == slot_rows[t][...]))
            theirs = hot((to >= SLOT) & (frm == to - SLOT + SLOT * line))
            for c in CHUNKS:
                value = dot(own, sources[t][:, c]) + dot(theirs, yrecv[t, :, c])
                blk[t, place, :, c] = value.astype(BF16)

    def out_copy(t, going_right, k, src, dst):
        way = 0 if going_right else 1
        return remote(
            blk.at[t, src],
            blk.at[t, dst],
            out_send_sem.at[t, way, k],
            out_recv_sem.at[t, dst],
            right if going_right else left,
        )

    def out_send(t, k, finish=False):
        for going_right in (True, False):
            plan = out_plan(going_right, k)
            if not any(p[0] for p in plan):
                continue
            active, src, dst = (pick(q, [int(p[i]) for p in plan]) for i in range(3))

            @pl.when(active == 1)
            def _():
                copy = out_copy(t, going_right, k, src, dst)
                if finish:
                    copy.wait_send()
                else:
                    copy.start()

    def out_arrive(t, k):
        for going_right in (True, False):
            plan = out_plan(going_right, k)
            plan = [plan[(i - 1) % 4] if going_right else plan[(i + 1) % 4] for i in range(4)]
            active, _, dst = (pick(q, [int(p[i]) for p in plan]) for i in range(3))

            @pl.when(active == 1)
            def _():
                out_copy(t, going_right, k, dst, dst).wait_recv()

    def cols(part):
        return pl.ds(part * HALF, HALF)

    def back_copy(t, part, going_left, k, src, dst):
        way = 0 if going_left else 1
        return remote(
            ret.at[t, src, :, cols(part)],
            ret.at[t, dst, :, cols(part)],
            back_send_sem.at[t, part, way, k],
            back_recv_sem.at[t, part, dst],
            left if going_left else right,
        )

    def back_send(t, part, k, finish=False):
        for going_left in (True, False):
            plan = back_plan(going_left, k)
            active, src, dst, added = (pick(q, [int(p[i]) for p in plan]) for i in range(4))
            if not finish and any(p[3] >= 0 for p in plan):

                @pl.when((active == 1) & (added >= 0))
                def _():
                    total = ret[t, src, :, cols(part)].astype(F32)
                    total = total + ret[t, added, :, cols(part)].astype(F32)
                    ret[t, src, :, cols(part)] = total.astype(BF16)

            @pl.when(active == 1)
            def _():
                copy = back_copy(t, part, going_left, k, src, dst)
                if finish:
                    copy.wait_send()
                else:
                    copy.start()

    def back_arrive(t, part, k):
        for going_left in (True, False):
            plan = back_plan(going_left, k)
            plan = [plan[(i + 1) % 4] if going_left else plan[(i - 1) % 4] for i in range(4)]
            active, _, dst, _ = (pick(q, [int(p[i]) for p in plan]) for i in range(4))

            @pl.when(active == 1)
            def _():
                back_copy(t, part, going_left, k, dst, dst).wait_recv()

    def pack(t, to):
        for c in CHUNKS:
            rows = [blk[t, i, :, c].astype(F32) for i in range(8)]
            to[:, c] = jnp.concatenate(rows, axis=0).astype(BF16)

    def spread(t, c, value):
        for i in range(8):
            ret[t, i, :, c] = value[i * PAIR : (i + 1) * PAIR].astype(BF16)

    def hidden_bwd():
        pack(0, packed)
        pack(1, packed_g)
        gate = dot(packed[...], w_gate[...])
        up = dot(packed[...], w_up[...])
        dh = dot_t(packed_g[...], w_down[...])
        s = jax.nn.sigmoid(gate)
        act_a[...] = (dh * up * s * (1.0 + gate * (1.0 - s))).astype(BF16)
        act_b[...] = (dh * gate * s).astype(BF16)

    def rows_bwd(chunks):
        for c in chunks:
            spread(0, c, dot_t(act_a[...], w_gate[c, :]) + dot_t(act_b[...], w_up[c, :]))

    def hidden_fwd():
        pack(2, packed)
        gate = dot(packed[...], w_gate[...])
        up = dot(packed[...], w_up[...])
        act_a[...] = (gate * jax.nn.sigmoid(gate) * up).astype(BF16)

    def rows_fwd(chunks):
        for c in chunks:
            spread(1, c, dot(act_a[...], w_down[:, c]))

    def y_back_copy(t):
        return remote(
            ysend_back.at[t], yrecv_back.at[t], y_send_sem.at[3 + t], y_recv_sem.at[3 + t], across
        )

    def finish_home(t):
        for c in CHUNKS:
            fin[t, 0, :, c] = ret[t, q + 2, :, c].astype(F32)
            fin[t, 1, :, c] = ret[t, HOME, :, c].astype(F32)

        @pl.when(q < 3)
        def _():
            for c in CHUNKS:
                fin[t, 0, :, c] += ret[t, RECV + q + 2, :, c].astype(F32)

        @pl.when(q > 0)
        def _():
            for c in CHUNKS:
                fin[t, 0, :, c] += ret[t, RECV + q + 3, :, c].astype(F32)

        to, frm = grid(PAIR, PAIR)
        main = hot((frm >= SLOT) & (to == frm - SLOT + SLOT * half))
        other = hot((frm >= SLOT) & (to == frm - SLOT + SLOT * (1 - half)))
        for c in CHUNKS:
            value = dot(main, fin[t, 0, :, c].astype(BF16))
            value = value + dot(other, fin[t, 1, :, c].astype(BF16))
            ysend_back[t, :, c] = value.astype(BF16)
        y_back_copy(t).start()

    def combine(t, base, slot_col, prob, out):
        y_back_copy(t).wait_recv()
        _, col = grid(TOK, PAIR)
        slots = slot_col[...]
        main = hot((col < SLOT) & (slots == (2 * plane + half) * SLOT + col))
        other = hot((col < SLOT) & (slots == (2 * plane + 1 - half) * SLOT + col))
        theirs = hot(slots == (1 - plane) * PAIR + col)
        scale = prob[...]
        for c in CHUNKS:
            value = dot(main, fin[t, 0, :, c].astype(BF16))
            value = value + dot(other, fin[t, 1, :, c].astype(BF16))
            value = value + dot(theirs, yrecv_back[t, :, c])
            out[:, c] = (base[:, c].astype(F32) + scale * value).astype(BF16)

    send_across(0)
    shift_g.wait_recv()
    send_across(1)
    build(0)
    out_send(0, 0)
    build(1)
    out_send(1, 0)
    shift_x.wait_recv()
    send_across(2)
    for k in range(1, STEPS):
        out_arrive(0, k - 1)
        out_send(0, k)
        out_arrive(1, k - 1)
        out_send(1, k)
    out_arrive(0, STEPS - 1)
    build(2)
    out_send(2, 0)
    for copy in weight_copies:
        copy.wait()
    out_arrive(1, STEPS - 1)

    hidden_bwd()
    out_arrive(2, 0)
    out_send(2, 1)
    rows_bwd(CHUNKS)
    back_send(0, 0, 0)
    back_send(0, 1, 0)
    for k in range(1, STEPS):
        out_arrive(2, k)
        if k + 1 < STEPS:
            out_send(2, k + 1)
        for part in (0, 1):
            back_arrive(0, part, k - 1)
            back_send(0, part, k)
    hidden_fwd()
    rows_fwd(CHUNKS)
    back_send(1, 0, 0)
    back_send(1, 1, 0)
    for part in (0, 1):
        back_arrive(0, part, STEPS - 1)
    finish_home(0)
    for k in range(1, STEPS):
        for part in (0, 1):
            back_arrive(1, part, k - 1)
            back_send(1, part, k)
        if k == 2:
            combine(0, g_rows, slot_b_col, prob_b, out_b)
    for part in (0, 1):
        back_arrive(1, part, STEPS - 1)
    finish_home(1)
    combine(1, x_rows, slot_f_col, prob_f, out_f)

    shift_g.wait_send()
    shift_x.wait_send()
    for t in range(3):
        y_copy(t).wait_send()
        for k in range(STEPS):
            out_send(t, k, finish=True)
    for t in range(2):
        y_back_copy(t).wait_send()
        for part in (0, 1):
            for k in range(STEPS):
                back_send(t, part, k, finish=True)


def slots_of(ids, probs, position):
    own = lax.dynamic_slice_in_dim(ids.reshape(-1, TOK), position, 1)[0]
    prob = lax.dynamic_slice_in_dim(probs.reshape(-1, TOK), position, 1)[0]
    place = jnp.arange(TOK)
    earlier = (own[None, :] == own[:, None]) & (place[None, :] < place[:, None])
    slot = own * SLOT + jnp.sum(earlier.astype(jnp.int32), axis=1)
    return slot[None, :], slot[:, None], prob.astype(F32)[:, None]


def on_device(
    held_fwd, ids_fwd, probs_fwd, saved_in, held_grad, ids_bwd, probs_bwd, w_gate, w_up, w_down
):
    position = lax.axis_index("expert")
    forward = slots_of(ids_fwd[0], probs_fwd[0], position)
    backward = slots_of(ids_bwd[0], probs_bwd[0], position)
    vmem = pl.BlockSpec(memory_space=pltpu.VMEM)
    hbm = pl.BlockSpec(memory_space=pl.ANY)
    rows = jax.ShapeDtypeStruct((TOK, D), BF16)
    fwd, grad = pl.pallas_call(
        kernel,
        out_shape=(rows, rows),
        in_specs=[vmem] * 9 + [hbm] * 3,
        out_specs=(vmem, vmem),
        scratch_shapes=[
            pltpu.VMEM((D, HID), BF16),
            pltpu.VMEM((D, HID), BF16),
            pltpu.VMEM((HID, D), BF16),
            pltpu.VMEM((TOK, D), BF16),
            pltpu.VMEM((TOK, D), BF16),
            pltpu.VMEM((3, PAIR, D), BF16),
            pltpu.VMEM((3, PAIR, D), BF16),
            pltpu.VMEM((3, 10, PAIR, D), BF16),
            pltpu.VMEM((2, 19, PAIR, D), BF16),
            pltpu.VMEM((2, PAIR, D), BF16),
            pltpu.VMEM((2, PAIR, D), BF16),
            pltpu.VMEM((8 * PAIR, D), BF16),
            pltpu.VMEM((8 * PAIR, D), BF16),
            pltpu.VMEM((8 * PAIR, HID), BF16),
            pltpu.VMEM((8 * PAIR, HID), BF16),
            pltpu.VMEM((2, 2, PAIR, D), F32),
            pltpu.SemaphoreType.DMA((3,)),
            pltpu.SemaphoreType.DMA((2,)),
            pltpu.SemaphoreType.DMA((2,)),
            pltpu.SemaphoreType.DMA((5,)),
            pltpu.SemaphoreType.DMA((5,)),
            pltpu.SemaphoreType.DMA((3, 2, STEPS)),
            pltpu.SemaphoreType.DMA((3, 10)),
            pltpu.SemaphoreType.DMA((2, 2, 2, STEPS)),
            pltpu.SemaphoreType.DMA((2, 2, 19)),
        ],
        compiler_params=pltpu.CompilerParams(
            collective_id=0, has_side_effects=True, vmem_limit_bytes=60 * 2**20
        ),
        cost_estimate=pl.CostEstimate(
            flops=7_050_000_000, bytes_accessed=12_000_000, transcendentals=300_000
        ),
        name="relay_experts",
    )(held_fwd[0], held_grad[0], saved_in[0], *forward, *backward, w_gate[0], w_up[0], w_down[0])
    return (fwd[None], grad[None])


def solution(mesh):
    return jax.shard_map(
        on_device,
        mesh=mesh,
        in_specs=(
            P("pipe", "expert", None),
            P("pipe", None),
            P("pipe", None),
            P("pipe", "expert", None),
            P("pipe", "expert", None),
            P("pipe", None),
            P("pipe", None),
            P("pipe", None, "expert"),
            P("pipe", None, "expert"),
            P("pipe", "expert", None),
        ),
        out_specs=(P("pipe", "expert", None), P("pipe", "expert", None)),
        check_vma=False,
    )
```

time: 534 us -> 222 us (0.42); the launches traced: 526 us -> 220 us
  waiting for transfers between devices: 351 us -> 0 us
  Pallas kernels: 0 us -> 207 us
  other arithmetic: 55.5 us -> 5.09 us
  local copies, waits for them, and re-layouts: 56.3 us -> 7.26 us
  matrix products: 30.4 us -> 0 us
  starting transfers between devices: 17.9 us -> 0 us
  between operations: 14.6 us -> 0.67 us
    all_gather x3 -> x0, waiting for transfers between devices: 305 us -> none  [the longest x1 110 us: on_device(): lax.all_gather(grads_in, 'expert', axis=0, tiled=True)]
    pallas_call x0 -> x1, Pallas kernels: none -> 207 us  [on_device(): pl.pallas_call(kernel, out_shape=(rows, rows), in_specs=[vmem] * 9 + [hbm...]
    gather x5 -> x0, local copies, waits for them, and re-layouts: 39.5 us -> none  [the longest x1 11.7 us: on_device(): grads_all[picked_back]]
    all_to_all x2 -> x0, waiting for transfers between devices: 34.6 us -> none  [the longest x1 34.6 us: on_device(): lax.all_to_all(back_rows, 'expert', split_axis=0, concat_axis=0, tiled=True)]
    dot_general x6 -> x0, matrix products: 30.4 us -> none  [the longest x1 7.48 us: expert_backward(): result = jnp.dot(d_gate, gate_cols.T, preferred_element_type=jnp.float32)]
    scatter-add x10 -> x0, other arithmetic: 16.1 us -> none  [the longest x2 8.17 us: combine_slots(): empty_rows.at[places_all.reshape(-1)]]
    all_to_all x2 -> x0, starting transfers between devices: 13.9 us -> none  [the longest x1 7.53 us: on_device(): lax.all_to_all(back_rows, 'expert', split_axis=0, concat_axis=0, tiled=True)]
    unnamed x8 -> x4, other arithmetic: 15.6 us -> 4.11 us
  transfers between devices with their start and end apart: 7 -> 0, of which waited for: 6 -> 0; matrix products, arithmetic and copies ran while one was open for 25% -> 0% of each run, Pallas kernels for 0% -> 0%
where the time goes in v1:
time: 222 us; the launch traced here: 220 us
  Pallas kernels  207 us (93%)
  local copies, waits for them, and re-layouts  7.26 us (3%)
  other arithmetic  5.09 us (2%)
    pallas_call x1, Pallas kernels, on_device(): pl.pallas_call(kernel, out_shape=(rows, rows), in_specs=[vmem] * 9 + [hbm...  207 us

profile of v1, /device:TPU:38, one launch (start us, length us, event | category | flops | bytes accessed | tf_op | source)
XLA Modules:
  0.0 220.4 jit_solution(10209914562395119898)
XLA Ops:
  0.6 0.7 reduce.1
  1.3 0.1 reshape_squeeze.13
  1.4 0.7 reduce.3
  2.1 0.1 reshape_squeeze.15
  2.2 0.5 broadcast.35
  2.7 1.3 reduce.8
  4.1 1.3 reduce.9
  5.4 0.1 reshape_squeeze.14
  5.5 0.2 convert_reduce_fusion
  5.7 0.1 reshape_squeeze.12
  5.8 0.2 convert_reduce_fusion.1
  6.0 0.6 bitcast_add_fusion.1
  6.6 0.7 copy.26.slot_b_col
  7.3 0.7 copy.25.prob_f
  8.0 0.7 copy.24.slot_f_col
  8.7 0.7 copy.27.prob_b
  9.4 207.4 %relay_experts.1 = (bf16[64,3584]{1,0:T(8,128)(2,1)}, bf16[64,3584]{1,0:T(8,128)(2,1)}) custom-call(bf16[64,3584]{1,0:T(8,128)(2,1)} %bitcast.39, bf16[64,3584]{1,0:T(8,128)(2,1)} %bitcast.40, bf16[64,3584]{1,0:T(8,128)(2,1)} %bitcast.41, s32[1,64]{1,0:T(1,128)} %get-tuple-element.11.slot_f_row, s32[64,1]{1,0:T(8,128)} %copy.24.slot_f_col, ...), custom_call_target="tpu_custom_call" | custom-call | flops 7049999872 | bytes 12000000 | tf_op jit(solution)/shard_map/relay_experts/pallas_call | solution.py:434
  216.8 1.8 copy.30
  218.6 1.8 copy.31
  (4 shorter events, 0.0 us)

commit v2 on v0

v2 whole, which is shorter than its diff:
```python
import jax
import jax.numpy as jnp
from jax import lax
from jax.experimental import pallas as pl
from jax.experimental.pallas import tpu as pltpu
from jax.sharding import PartitionSpec as P

SLOT = 20
MESH = pl.DeviceIdType.MESH
F32 = jnp.float32
BF16 = jnp.bfloat16

D = 3584
HID = 384
TOK = 64
ROWS = 2 * SLOT
HALF = D // 2
WIDE = 256
STARTS = tuple(range(0, HALF, WIDE))
ALL = 8 * SLOT
STEPS = 6

OTHER, PASS = 8, 9
RECV, HOME, TRANSIT = 8, 17, 18
S_A, G_A, S_B, G_B, X_B, X_A = range(6)
R_A, R_B, F_B, F_A = range(4)
PARTS = (1, 1, 1, 2)
DEPTH = 3

ORDER = (
    (
        (),
        (),
        ((0, 0, 0), (0, 1, 0)),
        ((0, 0, 1), (0, 1, 1), (2, 0, 0), (2, 1, 0), (0, 0, 2)),
        ((1, 0, 0), (1, 1, 0), (2, 0, 1), (1, 0, 1), (3, 1, 0), (2, 1, 1)),
        ((3, 0, 0), (5, 1, 0), (3, 0, 1), (2, 0, 2), (1, 1, 1), (4, 0, 0), (4, 1, 0)),
        ((5, 0, 0), (1, 0, 2), (4, 0, 1), (5, 0, 1), (3, 1, 1)),
        (),
        ((3, 0, 2),),
        (),
        (),
        (),
        (),
        (),
        (),
        (),
        (),
        ((6, 1, 0), (6, 1, 1)),
        ((6, 1, 2), (6, 1, 3), (4, 1, 1), (6, 1, 4)),
        (),
        ((4, 0, 2),),
        (),
        (),
        (),
        (),
        (),
        (),
        (),
        (),
        ((8, 1, 0), (8, 1, 1), (8, 1, 2), (8, 1, 3), (5, 1, 1), (8, 1, 4), (5, 0, 2)),
        (),
        (),
        (),
        (),
        (),
        ((8, 0, 3),),
        (),
        (),
        (),
        ((10, 1, 0), (10, 1, 1), (8, 0, 4), (10, 1, 2)),
        ((8, 1, 5), (10, 1, 3), (10, 1, 4)),
        (),
        (),
        (),
        (),
        (),
        ((10, 0, 3),),
        ((12, 1, 0), (12, 1, 1)),
        (),
        (),
        ((10, 0, 4), (13, 1, 0), (13, 1, 1), (10, 1, 5), (12, 1, 2)),
        (),
        ((6, 0, 3), (13, 1, 2), (6, 0, 4), (12, 1, 3), (13, 1, 3), (6, 1, 5), (12, 1, 4), (12, 0, 3)),
        ((13, 0, 3), (12, 0, 4), (13, 1, 4)),
        ((13, 0, 4), (12, 1, 5), (13, 1, 5)),
        (),
    ),
    (
        (),
        (),
        ((0, 0, 0), (0, 1, 0), (0, 1, 1)),
        ((0, 0, 1), (0, 1, 2), (2, 0, 0), (2, 1, 1), (0, 0, 2)),
        ((0, 1, 3), (1, 0, 0), (2, 1, 0), (2, 0, 1), (0, 1, 4), (0, 0, 3), (2, 1, 2)),
        ((2, 0, 2), (1, 1, 0), (1, 0, 1)),
        ((0, 1, 5), (1, 0, 2), (2, 1, 3), (3, 0, 0), (1, 1, 1), (3, 0, 1), (2, 1, 4), (2, 0, 3), (1, 1, 2), (3, 0, 2), (1, 1, 3), (4, 0, 0), (2, 1, 5), (1, 0, 3), (1, 1, 4), (4, 0, 1), (3, 1, 0), (4, 0, 2)),
        ((1, 1, 5),),
        (),
        ((5, 0, 0),),
        (),
        ((3, 1, 1),),
        (),
        (),
        ((5, 0, 1),),
        (),
        (),
        ((3, 1, 2),),
        ((5, 0, 2), (3, 1, 3), (3, 1, 4), (3, 0, 3), (4, 1, 0)),
        ((3, 1, 5), (6, 1, 1)),
        (),
        (),
        ((4, 1, 1), (6, 1, 2)),
        (),
        (),
        (),
        (),
        ((6, 1, 3), (4, 1, 2)),
        (),
        ((6, 1, 4), (4, 1, 3), (4, 1, 4), (4, 0, 3), (5, 1, 0), (8, 1, 1), (5, 1, 1)),
        (),
        (),
        ((8, 1, 2), (4, 1, 5)),
        (),
        (),
        (),
        (),
        (),
        ((8, 1, 3), (8, 0, 2)),
        ((8, 1, 4), (8, 0, 3), (8, 0, 4), (5, 0, 3), (5, 1, 2), (5, 1, 3), (10, 1, 1), (5, 1, 4), (10, 1, 2), (5, 1, 5), (10, 1, 3), (10, 0, 2)),
        (),
        (),
        ((10, 0, 3),),
        ((10, 1, 4),),
        (),
        (),
        (),
        ((10, 0, 4),),
        (),
        (),
        ((6, 0, 2), (12, 1, 1), (6, 0, 3), (12, 1, 2), (13, 1, 1), (6, 0, 4), (13, 1, 2), (12, 0, 2)),
        (),
        ((12, 1, 3), (13, 0, 2), (13, 1, 3), (12, 0, 3), (12, 1, 4), (13, 0, 3), (13, 1, 4), (12, 0, 4), (13, 0, 4)),
        (),
        (),
        (),
    ),
    (
        (),
        (),
        ((0, 0, 0), (0, 1, 0), (0, 0, 1)),
        ((0, 0, 2), (0, 1, 1), (2, 1, 0), (2, 0, 1), (0, 1, 2)),
        ((0, 0, 3), (1, 1, 0), (2, 0, 0), (2, 1, 1), (0, 0, 4), (0, 1, 3), (2, 0, 2)),
        ((2, 1, 2), (1, 0, 0), (1, 1, 1)),
        ((0, 0, 5), (1, 1, 2), (2, 0, 3), (3, 1, 0), (1, 0, 1), (3, 1, 1), (2, 0, 4), (2, 1, 3), (1, 0, 2), (3, 1, 2), (1, 0, 3), (4, 1, 0), (2, 0, 5), (1, 1, 3), (1, 0, 4), (4, 1, 1), (3, 0, 0), (4, 1, 2)),
        ((1, 0, 5),),
        (),
        ((5, 1, 0),),
        (),
        ((3, 0, 1),),
        (),
        (),
        ((5, 1, 1),),
        (),
        (),
        ((3, 0, 2),),
        ((5, 1, 2), (3, 0, 3), (3, 0, 4), (3, 1, 3), (4, 0, 0)),
        ((3, 0, 5), (6, 0, 1)),
        (),
        (),
        ((4, 0, 1), (6, 0, 2)),
        (),
        (),
        (),
        (),
        ((6, 0, 3), (4, 0, 2)),
        (),
        ((6, 0, 4), (4, 0, 3), (4, 0, 4), (4, 1, 3), (5, 0, 0), (8, 0, 1), (5, 0, 1)),
        (),
        ((8, 0, 2), (4, 0, 5)),
        (),
        (),
        (),
        (),
        (),
        (),
        ((8, 1, 2), (8, 0, 3)),
        ((8, 0, 4), (8, 1, 3), (8, 1, 4), (5, 1, 3), (5, 0, 2), (5, 0, 3), (10, 0, 1), (5, 0, 4), (10, 0, 2), (5, 0, 5), (10, 0, 3), (10, 1, 2)),
        (),
        (),
        ((10, 1, 3),),
        ((10, 0, 4),),
        (),
        (),
        (),
        ((10, 1, 4),),
        (),
        (),
        ((6, 1, 2), (12, 0, 1), (6, 1, 3), (12, 0, 2), (13, 0, 1), (6, 1, 4), (13, 0, 2), (12, 1, 2)),
        (),
        ((12, 0, 3), (13, 1, 2), (13, 0, 3), (12, 1, 3), (12, 0, 4), (13, 1, 3), (13, 0, 4), (12, 1, 4), (13, 1, 4)),
        (),
        (),
        (),
    ),
    (
        (),
        (),
        ((0, 0, 0), (0, 1, 0)),
        ((0, 0, 1), (0, 1, 1), (2, 1, 0), (2, 0, 0), (0, 1, 2)),
        ((1, 0, 0), (1, 1, 0), (2, 1, 1), (1, 1, 1), (3, 0, 0), (2, 0, 1)),
        ((3, 1, 0), (5, 0, 0), (3, 1, 1), (2, 1, 2), (1, 0, 1), (4, 1, 0), (4, 0, 0)),
        ((5, 1, 0), (1, 1, 2), (4, 1, 1), (5, 1, 1), (3, 0, 1)),
        (),
        ((3, 1, 2),),
        (),
        (),
        (),
        (),
        (),
        (),
        (),
        (),
        ((6, 0, 0), (6, 0, 1)),
        ((6, 0, 2), (6, 0, 3), (4, 0, 1), (6, 0, 4)),
        (),
        ((4, 1, 2),),
        (),
        (),
        (),
        (),
        (),
        (),
        (),
        (),
        ((8, 0, 0), (8, 0, 1), (8, 0, 2), (8, 0, 3), (5, 0, 1), (8, 0, 4), (5, 1, 2)),
        (),
        (),
        (),
        (),
        (),
        ((8, 1, 3),),
        (),
        (),
        (),
        ((10, 0, 0), (10, 0, 1), (8, 1, 4), (10, 0, 2)),
        ((8, 0, 5), (10, 0, 3), (10, 0, 4)),
        (),
        (),
        (),
        (),
        (),
        ((10, 1, 3),),
        ((12, 0, 0), (12, 0, 1)),
        (),
        (),
        ((10, 1, 4), (13, 0, 0), (13, 0, 1), (10, 0, 5), (12, 0, 2)),
        (),
        ((6, 1, 3), (13, 0, 2), (6, 1, 4), (12, 0, 3), (13, 0, 3), (6, 0, 5), (12, 0, 4), (12, 1, 3)),
        ((13, 1, 3), (12, 1, 4), (13, 0, 4)),
        ((13, 1, 4), (12, 0, 5), (13, 0, 5)),
        (),
    ),
)


def mirrored(index):
    return 7 - index if index < 8 else index


def out_plan(right, k):
    plan = []
    for q in range(4):
        place = q if right else 3 - q
        active, src, dst = False, 0, 0
        if place < 2 and k < place + 3:
            active, src = True, place - k + 2
            dst = src
        elif place == 2:
            active = True
            src, dst = (OTHER, PASS) if k == 0 else (5 - k, 5 - k)
        elif place == 3 and k < 2:
            active, src, dst = True, OTHER + k, 1 - k
        if not right:
            src, dst = mirrored(src), mirrored(dst)
        plan.append((active, src, dst))
    return plan


def back_plan(left, k):
    plan = []
    for q in range(4):
        place = q if left else 3 - q
        active, src, dst, added = False, 0, 0, -1
        if 3 - place <= k <= 4:
            index = k - 3 + place
            active = True
            src = index if left else 7 - index
            slot = RECV + index if left else 16 - index
            dst = slot if place > 0 else TRANSIT - index
            added = slot if place < 3 else -1
        elif place == 3 and k == 5:
            active, src, dst = True, TRANSIT, HOME
        plan.append((active, src, dst, added))
    return plan


def kernel(
    held_fwd,
    held_grad,
    saved,
    ids_f,
    probs_f,
    ids_b,
    probs_b,
    w_gate_hbm,
    w_up_hbm,
    w_down_hbm,
    out_f,
    out_b,
    w_gate,
    w_up,
    w_down,
    x_rows,
    g_rows,
    y_out,
    y_back,
    blk,
    ret,
    lhs,
    act,
    pre,
    total,
    gathering,
    scattering,
    w_sem,
    shift_send,
    shift_recv,
    y_send_sem,
    y_recv_sem,
    out_send_sem,
    out_recv_sem,
    back_send_sem,
    back_recv_sem,
):
    pipe = lax.axis_index("pipe")
    position = lax.axis_index("expert")
    plane = position // 8
    z = position % 8
    half = z // 4
    q = z % 4
    right = (pipe, plane * 8 + (z + 1) % 8)
    left = (pipe, plane * 8 + (z + 7) % 8)
    across = (pipe, (1 - plane) * 8 + z)
    after = ((pipe + 1) % 16, position)
    before = ((pipe + 15) % 16, position)

    barrier = pltpu.get_barrier_semaphore()
    for device in (right, left, across, after, before):
        pl.semaphore_signal(barrier, inc=1, device_id=device, device_id_type=MESH)

    weight_copies = [
        pltpu.make_async_copy(w_gate_hbm, w_gate, w_sem.at[0]),
        pltpu.make_async_copy(w_up_hbm, w_up, w_sem.at[1]),
        pltpu.make_async_copy(w_down_hbm, w_down, w_sem.at[2]),
    ]
    for copy in weight_copies:
        copy.start()

    def remote(src, dst, send_sem, recv_sem, device):
        return pltpu.make_async_remote_copy(
            src_ref=src,
            dst_ref=dst,
            send_sem=send_sem,
            recv_sem=recv_sem,
            device_id=device,
            device_id_type=MESH,
        )

    def grid(rows, cols):
        return (
            lax.broadcasted_iota(jnp.int32, (rows, cols), 0),
            lax.broadcasted_iota(jnp.int32, (rows, cols), 1),
        )

    def hot(mask):
        return jnp.where(mask, jnp.float32(1), jnp.float32(0)).astype(BF16)

    def dot(a, b):
        return jnp.dot(a, b, preferred_element_type=F32)

    def dot_t(a, b):
        return lax.dot_general(a, b, (((1,), (1,)), ((), ())), preferred_element_type=F32)

    def own_part(ref):
        base = pl.multiple_of((position // 2) * 128, 128)
        both = ref[:, pl.ds(base, 128)].astype(F32)
        return jnp.where(position % 2 == 0, both[:, :TOK], both[:, TOK:])

    def upright(row):
        i, j = grid(TOK, TOK)
        return jnp.sum(jnp.where(i == j, row, jnp.float32(0)), axis=1, keepdims=True)

    def routing(ids_ref, probs_ref):
        row = own_part(ids_ref)
        col = upright(row)
        i, j = grid(TOK, TOK)
        one, none = jnp.float32(1), jnp.float32(0)
        rank_row = jnp.sum(jnp.where((row == col) & (i < j), one, none), axis=0, keepdims=True)
        rank_col = jnp.sum(jnp.where((row == col) & (j < i), one, none), axis=1, keepdims=True)
        return row * SLOT + rank_row, col * SLOT + rank_col, upright(own_part(probs_ref))

    sources = (saved, g_rows, x_rows)

    def choose(t, slot_row):
        side = (S_A, G_A, X_A)[t]
        targets = (
            (2 * plane + half, blk.at[side, q + 2]),
            (2 * plane + 1 - half, blk.at[side, OTHER]),
            (2 * (1 - plane) + half, y_out.at[t, 0]),
            (2 * (1 - plane) + 1 - half, y_out.at[t, 1]),
        )
        i, j = grid(ROWS, 2 * TOK)
        slots = jnp.concatenate([slot_row, slot_row], axis=1)
        slots = jnp.where((i < SLOT) == (j < TOK), slots, jnp.float32(-1))
        offset = jnp.where(i < SLOT, i, i - SLOT)
        maps = [
            jnp.where((offset + expert * SLOT).astype(F32) == slots, jnp.float32(1), jnp.float32(0))
            for expert, _ in targets
        ]
        maps = jnp.concatenate(maps, axis=0).astype(BF16)
        for c in STARTS:
            upper = sources[t][:, c : c + WIDE]
            lower = sources[t][:, HALF + c : HALF + c + WIDE]
            value = dot(maps, jnp.concatenate([upper, lower], axis=0))
            for n in range(4):
                targets[n][1][:, c : c + WIDE] = value[n * ROWS : (n + 1) * ROWS].astype(BF16)

    def y_copy(t, n):
        side = (S_B, G_B, X_B)[t]
        place = q + 2 if n == 0 else OTHER
        return remote(
            y_out.at[t, n], blk.at[side, place], y_send_sem.at[t, n], y_recv_sem.at[t, n], across
        )

    def columns(t, p):
        if PARTS[t] == 1:
            return pl.ds(0, HALF)
        return pl.ds(0, 4 * WIDE) if p == 0 else pl.ds(4 * WIDE, 3 * WIDE)

    def out_copy(t, way, k, src, dst):
        return remote(
            blk.at[t, src],
            blk.at[t, dst],
            out_send_sem.at[t, way, k],
            out_recv_sem.at[t, dst],
            right if way == 0 else left,
        )

    def back_copy(t, p, way, k, src, dst):
        return remote(
            ret.at[t, src, :, columns(t, p)],
            ret.at[t, dst, :, columns(t, p)],
            back_send_sem.at[t, p, way, k],
            back_recv_sem.at[t, p, dst],
            left if way == 0 else right,
        )

    arrived = [set() for _ in range(4)]
    started = [([], []) for _ in range(4)]

    def need(place, key):
        if key in arrived[place]:
            return
        arrived[place].add(key)
        if key[0] == "out":
            out_copy(key[1], 0, 0, key[2], key[2]).wait_recv()
        elif key[0] == "back":
            back_copy(key[1], key[2], 0, 0, key[3], key[3]).wait_recv()
        elif key[1] in (S_B, G_B, X_B):
            y_copy((S_B, G_B, X_B).index(key[1]), key[2]).wait_recv()

    def described(place, op):
        stream, way, k = op
        if stream < 6:
            _, src, dst = out_plan(way == 0, k)[place]
            return out_copy(stream, way, k, src, dst)
        t, p = (stream - 6) // 2, (stream - 6) % 2
        _, src, dst, _ = back_plan(way == 0, k)[place]
        return back_copy(t, p, way, k, src, dst)

    def start(place, op):
        stream, way, k = op
        if stream < 6:
            _, src, _ = out_plan(way == 0, k)[place]
            if src == place + 2:
                need(place, ("own", stream, 0))
            elif src == OTHER:
                need(place, ("own", stream, 1))
            else:
                need(place, ("out", stream, src))
        else:
            t, p = (stream - 6) // 2, (stream - 6) % 2
            _, src, _, added = back_plan(way == 0, k)[place]
            if src == TRANSIT:
                need(place, ("back", t, p, TRANSIT))
            if added >= 0:
                need(place, ("back", t, p, added))
                cols = columns(t, p)
                joined = ret[t, src, :, cols].astype(F32) + ret[t, added, :, cols].astype(F32)
                ret[t, src, :, cols] = joined.astype(BF16)
        link = started[place][(way == 0) == (stream < 6)]
        if len(link) >= DEPTH:
            described(place, link[-DEPTH]).wait_send()
        link.append(op)
        described(place, op).start()

    def all_of(*sides):
        def keys(place):
            found = []
            for side in sides:
                found.append(("own", side, 0))
                found += [("out", side, i) for i in range(8) if i != place + 2]
            return found

        return keys

    def home_of(t, parts):
        def keys(place):
            found = []
            for p in parts:
                found.append(("back", t, p, HOME))
                if place < 3:
                    found.append(("back", t, p, RECV + place + 2))
                if place > 0:
                    found.append(("back", t, p, RECV + place + 3))
            return found

        return keys

    def nothing(place):
        return []

    count = [0]

    def piece(keys=nothing):
        number = count[0]
        count[0] += 1
        for place in range(4):
            ops = ORDER[place][number]
            if ops or any(key not in arrived[place] for key in keys(place)):

                @pl.when(q == place)
                def _():
                    for op in ops:
                        start(place, op)
                    for key in keys(place):
                        need(place, key)

    def gather(t, to):
        for c in STARTS:
            rows = [blk[t, i, :, c : c + WIDE].astype(F32) for i in range(8)]
            value = dot(gathering[...], jnp.concatenate(rows, axis=0).astype(BF16)).astype(BF16)
            lhs[to, :, c : c + WIDE] = value[:ALL]
            lhs[to, :, HALF + c : HALF + c + WIDE] = value[ALL:]

    def scatter(t, c, upper, lower):
        both = jnp.concatenate([upper, lower], axis=0).astype(BF16)
        value = dot(scattering[...], both)
        for i in range(8):
            ret[t, i, :, c : c + WIDE] = value[i * ROWS : (i + 1) * ROWS].astype(BF16)

    def hidden_bwd():
        pre[0] = dot(lhs[0], w_gate[...])
        piece()
        pre[1] = dot(lhs[0], w_up[...])
        piece()
        dh = dot_t(lhs[1], w_down[...])
        gate, up = pre[0], pre[1]
        s = jax.nn.sigmoid(gate)
        act[0] = (dh * up * s * (1.0 + gate * (1.0 - s))).astype(BF16)
        act[1] = (dh * gate * s).astype(BF16)

    def rows_bwd(t):
        for c in STARTS:
            piece()
            values = []
            for n in (slice(c, c + WIDE), slice(HALF + c, HALF + c + WIDE)):
                values.append(dot_t(act[0], w_gate[n, :]) + dot_t(act[1], w_up[n, :]))
            scatter(t, c, *values)

    def hidden_fwd():
        pre[0] = dot(lhs[0], w_gate[...])
        piece()
        gate = pre[0]
        up = dot(lhs[0], w_up[...])
        act[0] = (gate * jax.nn.sigmoid(gate) * up).astype(BF16)

    def rows_fwd(t):
        for c in STARTS:
            piece()
            upper = dot(act[0], w_down[:, c : c + WIDE])
            lower = dot(act[0], w_down[:, HALF + c : HALF + c + WIDE])
            scatter(t, c, upper, lower)

    def join_home(t, cols):
        place = q + 2

        def joined(*others):
            value = ret[t, place, :, cols].astype(F32)
            for other in others:
                value = value + ret[t, other, :, cols].astype(F32)
            ret[t, place, :, cols] = value.astype(BF16)

        pl.when(q == 0)(lambda: joined(RECV + place))
        pl.when((q > 0) & (q < 3))(lambda: joined(RECV + place, RECV + place + 1))
        pl.when(q == 3)(lambda: joined(RECV + place + 1))

    def y_back_copy(t, n):
        src = ret.at[(R_B, F_B)[t], q + 2 if n == 0 else HOME]
        return remote(
            src, y_back.at[t, n], y_send_sem.at[3 + t, n], y_recv_sem.at[3 + t, n], across
        )

    def home_b(t):
        join_home((R_B, F_B)[t], pl.ds(0, HALF))
        for n in (0, 1):
            y_back_copy(t, n).start()

    def combine(t, slot_col, owner, blocks, base, out, starts):
        i, j = grid(2 * TOK, 2 * ROWS)
        within = jnp.where(j < ROWS, j, j - ROWS)
        first = (2 * owner + jnp.where(j < ROWS, half, 1 - half)) * SLOT
        slot = first + jnp.where(within < SLOT, within, within - SLOT)
        slots = jnp.concatenate([slot_col, slot_col], axis=0)
        maps = hot((slot.astype(F32) == slots) & ((within < SLOT) == (i < TOK)))
        scale = probs_col[t]
        for c in starts:
            both = [block[:, c : c + WIDE].astype(F32) for block in blocks]
            value = dot(maps, jnp.concatenate(both, axis=0).astype(BF16))
            for n, at in ((slice(c, c + WIDE), 0), (slice(HALF + c, HALF + c + WIDE), TOK)):
                added = base[:, n].astype(F32) + scale * value[at : at + TOK]
                out[:, n] = added.astype(out.dtype)

    def combine_b(t):
        for n in (0, 1):
            y_back_copy(t, n).wait_recv()
        blocks = (y_back.at[t, 0], y_back.at[t, 1])
        combine(t, slot_cols[t], 1 - plane, blocks, (g_rows, x_rows)[t], total.at[t], STARTS)

    def combine_a(t, p=None):
        side = (R_A, F_A)[t]
        join_home(side, pl.ds(0, HALF) if p is None else columns(side, p))
        starts = STARTS if p is None or PARTS[side] == 1 else (STARTS[:4], STARTS[4:])[p]
        blocks = (ret.at[side, q + 2], ret.at[side, HOME])
        combine(t, slot_cols[t], plane, blocks, total.at[t], (out_b, out_f)[t], starts)

    shift_g = remote(held_grad, g_rows, shift_send.at[0], shift_recv.at[0], before)
    shift_x = remote(held_fwd, x_rows, shift_send.at[1], shift_recv.at[1], after)

    def cross(t):
        for n in (0, 1):
            y_copy(t, n).start()

    piece()
    slot_row_b, slot_col_b, prob_b = routing(ids_b, probs_b)
    choose(0, slot_row_b)
    pl.semaphore_wait(barrier, 5)
    shift_g.start()

    piece()
    piece()
    slot_row_f, slot_col_f, prob_f = routing(ids_f, probs_f)
    slot_cols = (slot_col_b, slot_col_f)
    probs_col = (prob_b, prob_f)
    for way, ref in ((0, gathering), (1, scattering)):
        i, j = grid(2 * ALL, 2 * ALL)
        packed, whole = (j, i) if way == 0 else (i, j)
        within = lax.rem(packed, ROWS)
        goal = lax.div(packed, ROWS) * SLOT + lax.rem(within, SLOT)
        goal = goal + jnp.where(within >= SLOT, ALL, 0)
        ref[...] = hot(goal == whole)
    cross(0)

    piece()
    shift_g.wait_recv()
    choose(1, slot_row_b)
    cross(1)
    shift_x.start()

    piece()
    shift_x.wait_recv()
    choose(2, slot_row_f)
    cross(2)

    for saved_side, grad_side, back in ((S_A, G_A, R_A), (S_B, G_B, R_B)):
        piece(all_of(saved_side))
        gather(saved_side, 0)
        piece(all_of(grad_side))
        gather(grad_side, 1)
        if back == R_A:
            for copy in weight_copies:
                copy.wait()
        piece()
        hidden_bwd()
        rows_bwd(back)

    piece(all_of(X_B))
    gather(X_B, 0)
    piece()
    hidden_fwd()
    rows_fwd(F_B)

    piece(home_of(R_B, range(PARTS[R_B])))
    home_b(0)

    piece(all_of(X_A))
    gather(X_A, 0)
    piece()
    hidden_fwd()
    rows_fwd(F_A)

    piece(home_of(F_B, range(PARTS[F_B])))
    home_b(1)
    piece()
    combine_b(0)
    piece(home_of(R_A, range(PARTS[R_A])))
    combine_a(0)
    piece()
    combine_b(1)
    for p in range(PARTS[F_A]):
        piece(home_of(F_A, (p,)))
        combine_a(1, p)

    shift_g.wait_send()
    shift_x.wait_send()
    for n in (0, 1):
        for t in range(3):
            y_copy(t, n).wait_send()
        for t in range(2):
            y_back_copy(t, n).wait_send()
    for place in range(4):

        @pl.when(q == place)
        def _():
            for link in started[place]:
                for op in link[-DEPTH:]:
                    described(place, op).wait_send()


def give(from_f, from_b, to_f, to_b):
    to_f[...] = from_f[...]
    to_b[...] = from_b[...]


def on_device(
    held_fwd, ids_fwd, probs_fwd, saved_in, held_grad, ids_bwd, probs_bwd, w_gate, w_up, w_down
):
    vmem = pl.BlockSpec(memory_space=pltpu.VMEM)
    hbm = pl.BlockSpec(memory_space=pl.ANY)
    rows = jax.ShapeDtypeStruct((TOK, D), BF16)
    fwd, grad = pl.pallas_call(
        kernel,
        out_shape=(rows, rows),
        in_specs=[vmem] * 7 + [hbm] * 3,
        out_specs=(vmem, vmem),
        scratch_shapes=[
            pltpu.VMEM((D, HID), BF16),
            pltpu.VMEM((D, HID), BF16),
            pltpu.VMEM((HID, D), BF16),
            pltpu.VMEM((TOK, D), BF16),
            pltpu.VMEM((TOK, D), BF16),
            pltpu.VMEM((3, 2, ROWS, HALF), BF16),
            pltpu.VMEM((2, 2, ROWS, HALF), BF16),
            pltpu.VMEM((6, 10, ROWS, HALF), BF16),
            pltpu.VMEM((4, 19, ROWS, HALF), BF16),
            pltpu.VMEM((2, ALL, D), BF16),
            pltpu.VMEM((2, ALL, HID), BF16),
            pltpu.VMEM((2, ALL, HID), F32),
            pltpu.VMEM((2, TOK, D), F32),
            pltpu.VMEM((2 * ALL, 2 * ALL), BF16),
            pltpu.VMEM((2 * ALL, 2 * ALL), BF16),
            pltpu.SemaphoreType.DMA((3,)),
            pltpu.SemaphoreType.DMA((2,)),
            pltpu.SemaphoreType.DMA((2,)),
            pltpu.SemaphoreType.DMA((5, 2)),
            pltpu.SemaphoreType.DMA((5, 2)),
            pltpu.SemaphoreType.DMA((6, 2, STEPS)),
            pltpu.SemaphoreType.DMA((6, 10)),
            pltpu.SemaphoreType.DMA((4, 2, 2, STEPS)),
            pltpu.SemaphoreType.DMA((4, 2, 19)),
        ],
        compiler_params=pltpu.CompilerParams(
            collective_id=0, has_side_effects=True, vmem_limit_bytes=60 * 2**20
        ),
        cost_estimate=pl.CostEstimate(
            flops=7_050_000_000, bytes_accessed=12_000_000, transcendentals=300_000
        ),
        name="relay_experts",
    )(
        held_fwd[0],
        held_grad[0],
        saved_in[0],
        ids_fwd,
        probs_fwd,
        ids_bwd,
        probs_bwd,
        w_gate[0],
        w_up[0],
        w_down[0],
    )
    fwd, grad = pl.pallas_call(
        give,
        out_shape=(rows, rows),
        in_specs=[vmem, vmem],
        out_specs=(vmem, vmem),
        name="give",
    )(fwd, grad)
    return (fwd[None], grad[None])


def solution(mesh):
    return jax.shard_map(
        on_device,
        mesh=mesh,
        in_specs=(
            P("pipe", "expert", None),
            P("pipe", None),
            P("pipe", None),
            P("pipe", "expert", None),
            P("pipe", "expert", None),
            P("pipe", None),
            P("pipe", None),
            P("pipe", None, "expert"),
            P("pipe", None, "expert"),
            P("pipe", "expert", None),
        ),
        out_specs=(P("pipe", "expert", None), P("pipe", "expert", None)),
        check_vma=False,
    )
```

time: 534 us -> 170 us (0.32); the launches traced: 526 us -> 170 us
  waiting for transfers between devices: 351 us -> 0 us
  Pallas kernels: 0 us -> 169 us
  local copies, waits for them, and re-layouts: 56.3 us -> 0 us
  other arithmetic: 55.5 us -> 0 us
  matrix products: 30.4 us -> 0 us
  starting transfers between devices: 17.9 us -> 0 us
  between operations: 14.6 us -> 0.64 us
    all_gather x3 -> x0, waiting for transfers between devices: 305 us -> none  [the longest x1 110 us: on_device(): lax.all_gather(grads_in, 'expert', axis=0, tiled=True)]
    pallas_call x0 -> x2, Pallas kernels: none -> 169 us  [the longest x1 167 us: on_device(): pl.pallas_call(kernel, out_shape=(rows, rows), in_specs=[vmem] * 7 + [hbm...]
    gather x5 -> x0, local copies, waits for them, and re-layouts: 39.5 us -> none  [the longest x1 11.7 us: on_device(): grads_all[picked_back]]
    all_to_all x2 -> x0, waiting for transfers between devices: 34.6 us -> none  [the longest x1 34.6 us: on_device(): lax.all_to_all(back_rows, 'expert', split_axis=0, concat_axis=0, tiled=True)]
    dot_general x6 -> x0, matrix products: 30.4 us -> none  [the longest x1 7.48 us: expert_backward(): result = jnp.dot(d_gate, gate_cols.T, preferred_element_type=jnp.float32)]
    scatter-add x10 -> x0, other arithmetic: 16.1 us -> none  [the longest x2 8.17 us: combine_slots(): empty_rows.at[places_all.reshape(-1)]]
    unnamed x8 -> x0, other arithmetic: 15.6 us -> none
    all_to_all x2 -> x0, starting transfers between devices: 13.9 us -> none  [the longest x1 7.53 us: on_device(): lax.all_to_all(back_rows, 'expert', split_axis=0, concat_axis=0, tiled=True)]
  transfers between devices with their start and end apart: 7 -> 0, of which waited for: 6 -> 0; matrix products, arithmetic and copies ran while one was open for 25% -> 0% of each run, Pallas kernels for 0% -> 0%
where the time goes in v2:
time: 170 us
  Pallas kernels  169 us (99%)
    pallas_call x1, Pallas kernels, on_device(): pl.pallas_call(kernel, out_shape=(rows, rows), in_specs=[vmem] * 7 + [hbm...  167 us

profile of v2, /device:TPU:38, one launch (start us, length us, event | category | flops | bytes accessed | tf_op | source)
XLA Modules:
  0.0 169.8 jit_solution(16323503616939811257)
XLA Ops:
  0.6 167.0 %relay_experts.1 = (bf16[64,3584]{1,0:T(8,128)(2,1)}, bf16[64,3584]{1,0:T(8,128)(2,1)}) custom-call(bf16[64,3584]{1,0:T(8,128)(2,1)} %bitcast.11, bf16[64,3584]{1,0:T(8,128)(2,1)} %bitcast.12, bf16[64,3584]{1,0:T(8,128)(2,1)} %bitcast.13, s32[1,1024]{1,0:T(1,128)} %ids_f.1, bf16[1,1024]{1,0:T(2,128)(2,1)} %probs_f.1, s32[1,1024]{1,0:T(1,128)} %ids_b.1, ...), custom_call_target="tpu_custom_call" | custom-call | flops 7049999872 | bytes 12000000 | tf_op jit(solution)/shard_map/relay_experts/pallas_call | solution.py:761
  167.7 2.1 %give.1 = (bf16[64,3584]{1,0:T(8,128)(2,1)}, bf16[64,3584]{1,0:T(8,128)(2,1)}) custom-call(bf16[64,3584]{1,0:T(8,128)(2,1)} %get-tuple-element.6.from_f, bf16[64,3584]{1,0:T(8,128)(2,1)} %get-tuple-element.7.from_b), custom_call_target="tpu_custom_call" | custom-call | tf_op jit(solution)/shard_map/give/pallas_call | solution.py:811

commit v3 on v2

--- a/solution.py
+++ b/solution.py
@@ -24,20 +24,22 @@
 RECV, HOME, TRANSIT = 8, 17, 18
 S_A, G_A, S_B, G_B, X_B, X_A = range(6)
 R_A, R_B, F_B, F_A = range(4)
-PARTS = (1, 1, 1, 2)
+PARTS = (2, 2, 2, 2)
 DEPTH = 3
+RAWS = (0, 1, 2)
+TENSOR = (0, 1, 0, 1, 2, 2)
 
 ORDER = (
     (
         (),
         (),
         ((0, 0, 0), (0, 1, 0)),
-        ((0, 0, 1), (0, 1, 1), (2, 0, 0), (2, 1, 0), (0, 0, 2)),
-        ((1, 0, 0), (1, 1, 0), (2, 0, 1), (1, 0, 1), (3, 1, 0), (2, 1, 1)),
-        ((3, 0, 0), (5, 1, 0), (3, 0, 1), (2, 0, 2), (1, 1, 1), (4, 0, 0), (4, 1, 0)),
-        ((5, 0, 0), (1, 0, 2), (4, 0, 1), (5, 0, 1), (3, 1, 1)),
-        (),
-        ((3, 0, 2),),
+        ((0, 0, 1), (2, 0, 0), (2, 1, 0)),
+        (),
+        ((1, 0, 0), (1, 1, 0)),
+        ((0, 1, 1), (2, 0, 1), (3, 0, 0), (1, 0, 1), (3, 1, 0)),
+        ((0, 0, 2), (5, 1, 0), (3, 0, 1)),
+        ((1, 1, 1), (2, 1, 1), (5, 0, 0), (4, 0, 0), (4, 1, 0), (1, 0, 2), (2, 0, 2), (3, 1, 1), (4, 0, 1), (3, 0, 2), (5, 0, 1)),
         (),
         (),
         (),
@@ -47,158 +49,170 @@
         (),
         (),
         ((6, 1, 0), (6, 1, 1)),
-        ((6, 1, 2), (6, 1, 3), (4, 1, 1), (6, 1, 4)),
-        (),
-        ((4, 0, 2),),
-        (),
-        (),
-        (),
-        (),
-        (),
-        (),
-        (),
-        (),
-        ((8, 1, 0), (8, 1, 1), (8, 1, 2), (8, 1, 3), (5, 1, 1), (8, 1, 4), (5, 0, 2)),
-        (),
-        (),
-        (),
-        (),
-        (),
-        ((8, 0, 3),),
-        (),
-        (),
-        (),
-        ((10, 1, 0), (10, 1, 1), (8, 0, 4), (10, 1, 2)),
-        ((8, 1, 5), (10, 1, 3), (10, 1, 4)),
-        (),
-        (),
-        (),
-        (),
+        (),
+        (),
+        (),
+        ((7, 1, 0), (5, 1, 1), (7, 1, 1)),
+        ((6, 1, 2), (7, 1, 2), (5, 0, 2), (6, 1, 3), (4, 1, 1), (7, 1, 3), (6, 1, 4), (4, 0, 2)),
+        (),
+        ((7, 1, 4),),
+        (),
+        (),
+        (),
+        (),
+        (),
+        ((8, 1, 0),),
+        ((8, 1, 1),),
+        (),
+        ((9, 1, 0), (9, 1, 1), (8, 1, 2), (6, 0, 3), (9, 1, 2), (7, 0, 3), (8, 1, 3), (9, 1, 3)),
+        (),
+        ((8, 1, 4),),
+        ((8, 0, 3), (9, 1, 4)),
+        (),
+        ((8, 0, 4),),
+        (),
+        ((10, 1, 0),),
+        (),
+        ((9, 0, 3),),
+        ((11, 1, 0), (9, 0, 4), (8, 1, 5), (10, 1, 1)),
+        ((9, 1, 5), (11, 1, 1), (10, 1, 2), (11, 1, 2), (10, 1, 3), (11, 1, 3), (6, 1, 5), (7, 1, 5)),
+        (),
+        ((10, 1, 4),),
+        ((6, 0, 4), (11, 1, 4)),
+        ((7, 0, 4),),
+        (),
+        (),
+        ((12, 1, 0),),
         (),
         ((10, 0, 3),),
-        ((12, 1, 0), (12, 1, 1)),
-        (),
-        (),
-        ((10, 0, 4), (13, 1, 0), (13, 1, 1), (10, 1, 5), (12, 1, 2)),
-        (),
-        ((6, 0, 3), (13, 1, 2), (6, 0, 4), (12, 1, 3), (13, 1, 3), (6, 1, 5), (12, 1, 4), (12, 0, 3)),
-        ((13, 0, 3), (12, 0, 4), (13, 1, 4)),
-        ((13, 0, 4), (12, 1, 5), (13, 1, 5)),
+        ((13, 1, 0), (11, 0, 3), (12, 1, 1), (13, 1, 1), (10, 1, 5), (10, 0, 4), (11, 1, 5), (11, 0, 4), (12, 1, 2), (13, 1, 2)),
+        (),
+        ((12, 0, 3), (12, 1, 3), (13, 1, 3)),
+        ((13, 0, 3), (12, 0, 4), (12, 1, 4), (13, 1, 4), (13, 0, 4), (12, 1, 5)),
+        ((13, 1, 5),),
         (),
     ),
     (
         (),
-        (),
-        ((0, 0, 0), (0, 1, 0), (0, 1, 1)),
-        ((0, 0, 1), (0, 1, 2), (2, 0, 0), (2, 1, 1), (0, 0, 2)),
-        ((0, 1, 3), (1, 0, 0), (2, 1, 0), (2, 0, 1), (0, 1, 4), (0, 0, 3), (2, 1, 2)),
-        ((2, 0, 2), (1, 1, 0), (1, 0, 1)),
-        ((0, 1, 5), (1, 0, 2), (2, 1, 3), (3, 0, 0), (1, 1, 1), (3, 0, 1), (2, 1, 4), (2, 0, 3), (1, 1, 2), (3, 0, 2), (1, 1, 3), (4, 0, 0), (2, 1, 5), (1, 0, 3), (1, 1, 4), (4, 0, 1), (3, 1, 0), (4, 0, 2)),
-        ((1, 1, 5),),
-        (),
-        ((5, 0, 0),),
-        (),
-        ((3, 1, 1),),
-        (),
-        (),
-        ((5, 0, 1),),
-        (),
-        (),
+        ((14, 1, 0),),
+        ((0, 0, 0),),
+        ((0, 0, 1), (0, 1, 2), (2, 0, 0), (0, 0, 2)),
+        (),
+        ((15, 1, 0), (1, 0, 0)),
+        ((0, 1, 3), (2, 0, 1), (1, 0, 1)),
+        ((2, 0, 2),),
+        ((0, 1, 4), (3, 0, 0), (1, 1, 2), (1, 0, 2), (1, 1, 3), (0, 0, 3), (16, 1, 0), (3, 0, 1), (1, 1, 4), (3, 0, 2)),
+        ((4, 0, 0), (1, 0, 3), (2, 0, 3), (0, 1, 5), (4, 0, 1), (2, 1, 2)),
+        (),
+        (),
+        ((1, 1, 5), (3, 0, 3)),
+        (),
+        (),
+        (),
+        (),
+        ((4, 0, 2),),
+        ((2, 1, 3),),
+        (),
+        (),
+        (),
+        ((5, 0, 0), (2, 1, 4)),
+        (),
+        (),
+        ((2, 1, 5), (5, 0, 1)),
+        (),
+        (),
+        (),
+        (),
+        ((5, 0, 2),),
         ((3, 1, 2),),
-        ((5, 0, 2), (3, 1, 3), (3, 1, 4), (3, 0, 3), (4, 1, 0)),
-        ((3, 1, 5), (6, 1, 1)),
-        (),
-        (),
-        ((4, 1, 1), (6, 1, 2)),
-        (),
-        (),
-        (),
-        (),
-        ((6, 1, 3), (4, 1, 2)),
-        (),
-        ((6, 1, 4), (4, 1, 3), (4, 1, 4), (4, 0, 3), (5, 1, 0), (8, 1, 1), (5, 1, 1)),
-        (),
-        (),
-        ((8, 1, 2), (4, 1, 5)),
-        (),
-        (),
-        (),
-        (),
-        (),
-        ((8, 1, 3), (8, 0, 2)),
-        ((8, 1, 4), (8, 0, 3), (8, 0, 4), (5, 0, 3), (5, 1, 2), (5, 1, 3), (10, 1, 1), (5, 1, 4), (10, 1, 2), (5, 1, 5), (10, 1, 3), (10, 0, 2)),
-        (),
-        (),
-        ((10, 0, 3),),
-        ((10, 1, 4),),
-        (),
-        (),
-        (),
-        ((10, 0, 4),),
-        (),
-        (),
-        ((6, 0, 2), (12, 1, 1), (6, 0, 3), (12, 1, 2), (13, 1, 1), (6, 0, 4), (13, 1, 2), (12, 0, 2)),
-        (),
-        ((12, 1, 3), (13, 0, 2), (13, 1, 3), (12, 0, 3), (12, 1, 4), (13, 0, 3), (13, 1, 4), (12, 0, 4), (13, 0, 4)),
-        (),
+        (),
+        ((3, 1, 3), (6, 1, 1), (6, 1, 2), (3, 1, 4), (7, 1, 1), (3, 1, 5), (7, 1, 2), (6, 1, 3), (7, 1, 3), (4, 1, 2), (5, 0, 3), (4, 1, 3), (6, 1, 4), (7, 1, 4), (4, 1, 4), (6, 0, 2), (4, 0, 3), (7, 0, 2), (8, 1, 1)),
+        ((4, 1, 5), (8, 1, 2)),
+        ((9, 1, 1), (8, 0, 2)),
+        ((9, 1, 2),),
+        (),
+        (),
+        ((8, 0, 3), (8, 1, 3)),
+        (),
+        (),
+        ((9, 1, 3), (9, 0, 2)),
+        ((8, 1, 4), (9, 0, 3), (9, 1, 4), (8, 0, 4), (9, 0, 4), (5, 1, 2), (5, 1, 3), (10, 1, 1), (11, 1, 1), (5, 1, 4), (10, 1, 2), (5, 1, 5)),
+        (),
+        ((11, 1, 2),),
+        (),
+        ((6, 0, 3), (10, 1, 3)),
+        (),
+        ((11, 1, 3),),
+        (),
+        (),
+        (),
+        (),
+        ((7, 0, 3), (10, 1, 4), (11, 1, 4), (10, 0, 2), (11, 0, 2), (6, 0, 4), (7, 0, 4), (10, 0, 3), (11, 0, 3), (12, 1, 1), (13, 1, 1), (10, 0, 4), (11, 0, 4), (12, 1, 2), (13, 1, 2), (12, 0, 2), (13, 0, 2)),
+        ((12, 0, 3),),
+        ((12, 1, 3), (13, 0, 3)),
+        ((13, 1, 3), (12, 1, 4), (12, 0, 4), (13, 1, 4), (13, 0, 4)),
         (),
         (),
     ),
     (
         (),
-        (),
-        ((0, 0, 0), (0, 1, 0), (0, 0, 1)),
-        ((0, 0, 2), (0, 1, 1), (2, 1, 0), (2, 0, 1), (0, 1, 2)),
-        ((0, 0, 3), (1, 1, 0), (2, 0, 0), (2, 1, 1), (0, 0, 4), (0, 1, 3), (2, 0, 2)),
-        ((2, 1, 2), (1, 0, 0), (1, 1, 1)),
-        ((0, 0, 5), (1, 1, 2), (2, 0, 3), (3, 1, 0), (1, 0, 1), (3, 1, 1), (2, 0, 4), (2, 1, 3), (1, 0, 2), (3, 1, 2), (1, 0, 3), (4, 1, 0), (2, 0, 5), (1, 1, 3), (1, 0, 4), (4, 1, 1), (3, 0, 0), (4, 1, 2)),
-        ((1, 0, 5),),
-        (),
-        ((5, 1, 0),),
-        (),
-        ((3, 0, 1),),
-        (),
-        (),
-        ((5, 1, 1),),
-        (),
-        (),
+        ((14, 0, 0),),
+        ((0, 1, 0),),
+        ((0, 1, 1), (0, 0, 2), (2, 1, 0), (0, 1, 2)),
+        (),
+        ((15, 0, 0), (1, 1, 0)),
+        ((0, 0, 3), (2, 1, 1), (1, 1, 1)),
+        ((2, 1, 2),),
+        ((0, 0, 4), (3, 1, 0), (1, 0, 2), (1, 1, 2), (1, 0, 3), (0, 1, 3), (16, 0, 0), (3, 1, 1), (1, 0, 4), (3, 1, 2)),
+        ((4, 1, 0), (1, 1, 3), (2, 1, 3), (0, 0, 5), (4, 1, 1), (2, 0, 2)),
+        (),
+        (),
+        ((3, 1, 3), (1, 0, 5)),
+        (),
+        (),
+        (),
+        (),
+        ((4, 1, 2),),
+        ((2, 0, 3),),
+        (),
+        (),
+        (),
+        ((5, 1, 0), (2, 0, 4)),
+        (),
+        (),
+        ((5, 1, 1), (2, 0, 5)),
+        (),
+        (),
+        (),
+        (),
+        ((5, 1, 2),),
         ((3, 0, 2),),
-        ((5, 1, 2), (3, 0, 3), (3, 0, 4), (3, 1, 3), (4, 0, 0)),
-        ((3, 0, 5), (6, 0, 1)),
-        (),
-        (),
-        ((4, 0, 1), (6, 0, 2)),
-        (),
-        (),
-        (),
-        (),
-        ((6, 0, 3), (4, 0, 2)),
-        (),
-        ((6, 0, 4), (4, 0, 3), (4, 0, 4), (4, 1, 3), (5, 0, 0), (8, 0, 1), (5, 0, 1)),
-        (),
-        ((8, 0, 2), (4, 0, 5)),
-        (),
-        (),
-        (),
-        (),
-        (),
-        (),
-        ((8, 1, 2), (8, 0, 3)),
-        ((8, 0, 4), (8, 1, 3), (8, 1, 4), (5, 1, 3), (5, 0, 2), (5, 0, 3), (10, 0, 1), (5, 0, 4), (10, 0, 2), (5, 0, 5), (10, 0, 3), (10, 1, 2)),
-        (),
-        (),
-        ((10, 1, 3),),
-        ((10, 0, 4),),
-        (),
-        (),
-        (),
-        ((10, 1, 4),),
-        (),
-        (),
-        ((6, 1, 2), (12, 0, 1), (6, 1, 3), (12, 0, 2), (13, 0, 1), (6, 1, 4), (13, 0, 2), (12, 1, 2)),
-        (),
-        ((12, 0, 3), (13, 1, 2), (13, 0, 3), (12, 1, 3), (12, 0, 4), (13, 1, 3), (13, 0, 4), (12, 1, 4), (13, 1, 4)),
-        (),
+        (),
+        ((3, 0, 3), (6, 0, 1), (6, 0, 2), (3, 0, 4), (7, 0, 1), (3, 0, 5), (7, 0, 2), (6, 0, 3), (7, 0, 3), (4, 0, 2), (5, 1, 3), (4, 0, 3), (6, 0, 4), (7, 0, 4), (4, 0, 4), (6, 1, 2), (4, 1, 3), (7, 1, 2), (8, 0, 1)),
+        ((4, 0, 5), (8, 0, 2)),
+        ((9, 0, 1), (8, 1, 2)),
+        ((9, 0, 2),),
+        (),
+        (),
+        ((8, 1, 3), (8, 0, 3)),
+        (),
+        (),
+        ((9, 0, 3), (9, 1, 2)),
+        ((8, 0, 4), (9, 1, 3), (9, 0, 4), (8, 1, 4), (9, 1, 4), (5, 0, 2), (5, 0, 3), (10, 0, 1), (11, 0, 1), (5, 0, 4), (10, 0, 2), (5, 0, 5)),
+        (),
+        ((11, 0, 2),),
+        (),
+        ((6, 1, 3), (10, 0, 3)),
+        (),
+        ((11, 0, 3),),
+        (),
+        (),
+        (),
+        (),
+        ((7, 1, 3), (10, 0, 4), (11, 0, 4), (10, 1, 2), (11, 1, 2), (6, 1, 4), (7, 1, 4), (10, 1, 3), (11, 1, 3), (12, 0, 1), (13, 0, 1), (10, 1, 4), (11, 1, 4), (12, 0, 2), (13, 0, 2), (12, 1, 2), (13, 1, 2)),
+        ((12, 1, 3),),
+        ((12, 0, 3), (13, 1, 3)),
+        ((13, 0, 3), (12, 0, 4), (12, 1, 4), (13, 0, 4), (13, 1, 4)),
         (),
         (),
     ),
@@ -206,12 +220,12 @@
         (),
         (),
         ((0, 0, 0), (0, 1, 0)),
-        ((0, 0, 1), (0, 1, 1), (2, 1, 0), (2, 0, 0), (0, 1, 2)),
-        ((1, 0, 0), (1, 1, 0), (2, 1, 1), (1, 1, 1), (3, 0, 0), (2, 0, 1)),
-        ((3, 1, 0), (5, 0, 0), (3, 1, 1), (2, 1, 2), (1, 0, 1), (4, 1, 0), (4, 0, 0)),
-        ((5, 1, 0), (1, 1, 2), (4, 1, 1), (5, 1, 1), (3, 0, 1)),
-        (),
-        ((3, 1, 2),),
+        ((0, 1, 1), (2, 1, 0), (2, 0, 0)),
+        (),
+        ((1, 0, 0), (1, 1, 0)),
+        ((0, 0, 1), (2, 1, 1), (3, 1, 0), (1, 1, 1), (3, 0, 0)),
+        ((0, 1, 2), (5, 0, 0), (3, 1, 1)),
+        ((1, 0, 1), (2, 0, 1), (5, 1, 0), (4, 1, 0), (4, 0, 0), (1, 1, 2), (2, 1, 2), (3, 0, 1), (4, 1, 1), (3, 1, 2), (5, 1, 1)),
         (),
         (),
         (),
@@ -221,43 +235,47 @@
         (),
         (),
         ((6, 0, 0), (6, 0, 1)),
-        ((6, 0, 2), (6, 0, 3), (4, 0, 1), (6, 0, 4)),
-        (),
-        ((4, 1, 2),),
-        (),
-        (),
-        (),
-        (),
-        (),
-        (),
-        (),
-        (),
-        ((8, 0, 0), (8, 0, 1), (8, 0, 2), (8, 0, 3), (5, 0, 1), (8, 0, 4), (5, 1, 2)),
-        (),
-        (),
-        (),
-        (),
-        (),
-        ((8, 1, 3),),
-        (),
-        (),
-        (),
-        ((10, 0, 0), (10, 0, 1), (8, 1, 4), (10, 0, 2)),
-        ((8, 0, 5), (10, 0, 3), (10, 0, 4)),
-        (),
-        (),
-        (),
-        (),
+        (),
+        (),
+        (),
+        ((7, 0, 0), (5, 0, 1), (7, 0, 1)),
+        ((6, 0, 2), (7, 0, 2), (5, 1, 2), (6, 0, 3), (4, 0, 1), (7, 0, 3), (6, 0, 4), (4, 1, 2)),
+        (),
+        ((7, 0, 4),),
+        (),
+        (),
+        (),
+        (),
+        (),
+        ((8, 0, 0),),
+        ((8, 0, 1),),
+        (),
+        ((9, 0, 0), (9, 0, 1), (8, 0, 2), (6, 1, 3), (9, 0, 2), (7, 1, 3), (8, 0, 3), (9, 0, 3)),
+        (),
+        ((8, 0, 4),),
+        ((8, 1, 3), (9, 0, 4)),
+        (),
+        ((8, 1, 4),),
+        (),
+        ((10, 0, 0),),
+        (),
+        ((9, 1, 3),),
+        ((11, 0, 0), (9, 1, 4), (8, 0, 5), (10, 0, 1)),
+        ((9, 0, 5), (11, 0, 1), (10, 0, 2), (11, 0, 2), (10, 0, 3), (11, 0, 3), (6, 0, 5), (7, 0, 5)),
+        (),
+        ((10, 0, 4),),
+        ((6, 1, 4), (11, 0, 4)),
+        ((7, 1, 4),),
+        (),
+        (),
+        ((12, 0, 0),),
         (),
         ((10, 1, 3),),
-        ((12, 0, 0), (12, 0, 1)),
-        (),
-        (),
-        ((10, 1, 4), (13, 0, 0), (13, 0, 1), (10, 0, 5), (12, 0, 2)),
-        (),
-        ((6, 1, 3), (13, 0, 2), (6, 1, 4), (12, 0, 3), (13, 0, 3), (6, 0, 5), (12, 0, 4), (12, 1, 3)),
-        ((13, 1, 3), (12, 1, 4), (13, 0, 4)),
-        ((13, 1, 4), (12, 0, 5), (13, 0, 5)),
+        ((13, 0, 0), (11, 1, 3), (12, 0, 1), (13, 0, 1), (10, 0, 5), (10, 1, 4), (11, 0, 5), (11, 1, 4), (12, 0, 2), (13, 0, 2)),
+        (),
+        ((12, 0, 3), (12, 1, 3), (13, 0, 3)),
+        ((13, 1, 3), (12, 0, 4), (12, 1, 4), (13, 0, 4), (13, 1, 4), (12, 0, 5)),
+        ((13, 0, 5),),
         (),
     ),
 )
@@ -324,6 +342,8 @@
     g_rows,
     y_out,
     y_back,
+    raw,
+    edge_out,
     blk,
     ret,
     lhs,
@@ -337,6 +357,10 @@
     shift_recv,
     y_send_sem,
     y_recv_sem,
+    raw_send_sem,
+    raw_recv_sem,
+    edge_send_sem,
+    edge_recv_sem,
     out_send_sem,
     out_recv_sem,
     back_send_sem,
@@ -391,7 +415,7 @@
     def dot_t(a, b):
         return lax.dot_general(a, b, (((1,), (1,)), ((), ())), preferred_element_type=F32)
 
-    def own_part(ref):
+    def part_of(ref, position):
         base = pl.multiple_of((position // 2) * 128, 128)
         both = ref[:, pl.ds(base, 128)].astype(F32)
         return jnp.where(position % 2 == 0, both[:, :TOK], both[:, TOK:])
@@ -400,40 +424,63 @@
         i, j = grid(TOK, TOK)
         return jnp.sum(jnp.where(i == j, row, jnp.float32(0)), axis=1, keepdims=True)
 
-    def routing(ids_ref, probs_ref):
-        row = own_part(ids_ref)
+    def routing(ids_ref, probs_ref, position):
+        row = part_of(ids_ref, position)
         col = upright(row)
         i, j = grid(TOK, TOK)
         one, none = jnp.float32(1), jnp.float32(0)
         rank_row = jnp.sum(jnp.where((row == col) & (i < j), one, none), axis=0, keepdims=True)
         rank_col = jnp.sum(jnp.where((row == col) & (j < i), one, none), axis=1, keepdims=True)
-        return row * SLOT + rank_row, col * SLOT + rank_col, upright(own_part(probs_ref))
+        return row * SLOT + rank_row, col * SLOT + rank_col, upright(part_of(probs_ref, position))
 
     sources = (saved, g_rows, x_rows)
 
-    def choose(t, slot_row):
-        side = (S_A, G_A, X_A)[t]
-        targets = (
-            (2 * plane + half, blk.at[side, q + 2]),
-            (2 * plane + 1 - half, blk.at[side, OTHER]),
-            (2 * (1 - plane) + half, y_out.at[t, 0]),
-            (2 * (1 - plane) + 1 - half, y_out.at[t, 1]),
-        )
+    def choose(rows, slot_row, blocks):
+        experts = [2 * side + line for side in (plane, 1 - plane) for line in (half, 1 - half)]
         i, j = grid(ROWS, 2 * TOK)
         slots = jnp.concatenate([slot_row, slot_row], axis=1)
         slots = jnp.where((i < SLOT) == (j < TOK), slots, jnp.float32(-1))
         offset = jnp.where(i < SLOT, i, i - SLOT)
         maps = [
             jnp.where((offset + expert * SLOT).astype(F32) == slots, jnp.float32(1), jnp.float32(0))
-            for expert, _ in targets
+            for expert in experts
         ]
         maps = jnp.concatenate(maps, axis=0).astype(BF16)
         for c in STARTS:
-            upper = sources[t][:, c : c + WIDE]
-            lower = sources[t][:, HALF + c : HALF + c + WIDE]
+            upper = rows[:, c : c + WIDE]
+            lower = rows[:, HALF + c : HALF + c + WIDE]
             value = dot(maps, jnp.concatenate([upper, lower], axis=0))
             for n in range(4):
-                targets[n][1][:, c : c + WIDE] = value[n * ROWS : (n + 1) * ROWS].astype(BF16)
+                blocks[n][:, c : c + WIDE] = value[n * ROWS : (n + 1) * ROWS].astype(BF16)
+
+    on_edge = (q == 0) | (q == 3)
+    near = jnp.where(q == 3, 4, 3)
+
+    def choose_own(t, slot_row):
+        side = (S_A, G_A, X_A)[t]
+        blocks = (blk.at[side, q + 2], blk.at[side, OTHER], y_out.at[t, 0], y_out.at[t, 1])
+        choose(sources[t], slot_row, blocks)
+
+    def choose_near(t, slot_row):
+        side = (S_A, G_A, X_A)[t]
+        blocks = (blk.at[side, near], blk.at[side, PASS], edge_out.at[t, 0], edge_out.at[t, 1])
+        choose(raw.at[t], slot_row, blocks)
+
+    def edge_copy(t, n):
+        side = (S_B, G_B, X_B)[t]
+        place = near if n == 0 else PASS
+        return remote(
+            edge_out.at[t, n],
+            blk.at[side, place],
+            edge_send_sem.at[t, n],
+            edge_recv_sem.at[t, n],
+            across,
+        )
+
+    def raw_copy(t, way):
+        return remote(
+            sources[t], raw.at[t], raw_send_sem.at[t], raw_recv_sem.at[t], right if way == 0 else left
+        )
 
     def y_copy(t, n):
         side = (S_B, G_B, X_B)[t]
@@ -472,15 +519,23 @@
         if key in arrived[place]:
             return
         arrived[place].add(key)
-        if key[0] == "out":
+        picked = key[0] == "out" and place in (0, 3) and TENSOR[key[1]] in RAWS
+        if key[0] == "raw":
+            raw_copy(key[1], 0).wait_recv()
+        elif picked and key[2] in (4 if place == 3 else 3, PASS):
+            if key[1] in (S_B, G_B, X_B):
+                edge_copy(TENSOR[key[1]], 0 if key[2] < 8 else 1).wait_recv()
+        elif key[0] == "out":
             out_copy(key[1], 0, 0, key[2], key[2]).wait_recv()
         elif key[0] == "back":
             back_copy(key[1], key[2], 0, 0, key[3], key[3]).wait_recv()
         elif key[1] in (S_B, G_B, X_B):
-            y_copy((S_B, G_B, X_B).index(key[1]), key[2]).wait_recv()
+            y_copy(TENSOR[key[1]], key[2]).wait_recv()
 
     def described(place, op):
         stream, way, k = op
+        if stream >= 14:
+            return raw_copy(stream - 14, way)
         if stream < 6:
             _, src, dst = out_plan(way == 0, k)[place]
             return out_copy(stream, way, k, src, dst)
@@ -498,7 +553,7 @@
                 need(place, ("own", stream, 1))
             else:
                 need(place, ("out", stream, src))
-        else:
+        elif stream < 14:
             t, p = (stream - 6) // 2, (stream - 6) % 2
             _, src, _, added = back_plan(way == 0, k)[place]
             if src == TRANSIT:
@@ -508,7 +563,7 @@
                 cols = columns(t, p)
                 joined = ret[t, src, :, cols].astype(F32) + ret[t, added, :, cols].astype(F32)
                 ret[t, src, :, cols] = joined.astype(BF16)
-        link = started[place][(way == 0) == (stream < 6)]
+        link = started[place][(way == 0) == (stream < 6 or stream >= 14)]
         if len(link) >= DEPTH:
             described(place, link[-DEPTH]).wait_send()
         link.append(op)
@@ -657,19 +712,42 @@
     shift_g = remote(held_grad, g_rows, shift_send.at[0], shift_recv.at[0], before)
     shift_x = remote(held_fwd, x_rows, shift_send.at[1], shift_recv.at[1], after)
 
+    def crossing(t, act):
+        act(y_copy(t, 0))
+        if t in RAWS:
+            pl.when(on_edge)(lambda: act(y_copy(t, 1)))
+        else:
+            act(y_copy(t, 1))
+
     def cross(t):
-        for n in (0, 1):
-            y_copy(t, n).start()
+        crossing(t, lambda copy: copy.start())
+
+    def raw_of(t):
+        return lambda place: [("raw", t)] if place in (0, 3) else []
+
+    def pick_near(t):
+        if t not in RAWS:
+            return
+        piece(raw_of(t))
+
+        @pl.when(on_edge)
+        def _():
+            choose_near(t, (near_b, near_b, near_f)[t])
+            for n in (0, 1):
+                edge_copy(t, n).start()
 
     piece()
-    slot_row_b, slot_col_b, prob_b = routing(ids_b, probs_b)
-    choose(0, slot_row_b)
+    slot_row_b, slot_col_b, prob_b = routing(ids_b, probs_b, position)
+    choose_own(0, slot_row_b)
     pl.semaphore_wait(barrier, 5)
     shift_g.start()
 
     piece()
     piece()
-    slot_row_f, slot_col_f, prob_f = routing(ids_f, probs_f)
+    slot_row_f, slot_col_f, prob_f = routing(ids_f, probs_f, position)
+    neighbour = position + jnp.where(q == 0, 1, 0) - jnp.where(q == 3, 1, 0)
+    near_b = routing(ids_b, probs_b, neighbour)[0]
+    near_f = routing(ids_f, probs_f, neighbour)[0]
     slot_cols = (slot_col_b, slot_col_f)
     probs_col = (prob_b, prob_f)
     for way, ref in ((0, gathering), (1, scattering)):
@@ -683,14 +761,18 @@
 
     piece()
     shift_g.wait_recv()
-    choose(1, slot_row_b)
+
+    piece()
+    choose_own(1, slot_row_b)
     cross(1)
     shift_x.start()
+    pick_near(0)
 
     piece()
     shift_x.wait_recv()
-    choose(2, slot_row_f)
+    choose_own(2, slot_row_f)
     cross(2)
+    pick_near(1)
 
     for saved_side, grad_side, back in ((S_A, G_A, R_A), (S_B, G_B, R_B)):
         piece(all_of(saved_side))
@@ -703,6 +785,8 @@
         piece()
         hidden_bwd()
         rows_bwd(back)
+        if back == R_A:
+            pick_near(2)
 
     piece(all_of(X_B))
     gather(X_B, 0)
@@ -733,11 +817,14 @@
 
     shift_g.wait_send()
     shift_x.wait_send()
-    for n in (0, 1):
-        for t in range(3):
-            y_copy(t, n).wait_send()
-        for t in range(2):
+    for t in range(3):
+        crossing(t, lambda copy: copy.wait_send())
+    for t in range(2):
+        for n in (0, 1):
             y_back_copy(t, n).wait_send()
+    for t in RAWS:
+        for n in (0, 1):
+            pl.when(on_edge)(lambda: edge_copy(t, n).wait_send())
     for place in range(4):
 
         @pl.when(q == place)
@@ -771,6 +858,8 @@
             pltpu.VMEM((TOK, D), BF16),
             pltpu.VMEM((3, 2, ROWS, HALF), BF16),
             pltpu.VMEM((2, 2, ROWS, HALF), BF16),
+            pltpu.VMEM((3, TOK, D), BF16),
+            pltpu.VMEM((3, 2, ROWS, HALF), BF16),
             pltpu.VMEM((6, 10, ROWS, HALF), BF16),
             pltpu.VMEM((4, 19, ROWS, HALF), BF16),
             pltpu.VMEM((2, ALL, D), BF16),
@@ -784,6 +873,10 @@
             pltpu.SemaphoreType.DMA((2,)),
             pltpu.SemaphoreType.DMA((5, 2)),
             pltpu.SemaphoreType.DMA((5, 2)),
+            pltpu.SemaphoreType.DMA((3,)),
+            pltpu.SemaphoreType.DMA((3,)),
+            pltpu.SemaphoreType.DMA((3, 2)),
+            pltpu.SemaphoreType.DMA((3, 2)),
             pltpu.SemaphoreType.DMA((6, 2, STEPS)),
             pltpu.SemaphoreType.DMA((6, 10)),
             pltpu.SemaphoreType.DMA((4, 2, 2, STEPS)),

time: 170 us -> 165 us (0.971)
  Pallas kernels: 169 us -> 164 us
    pallas_call x1, Pallas kernels: 167 us -> 162 us  [on_device(): pl.pallas_call(kernel, out_shape=(rows, rows), in_specs=[vmem] * 7 + [hbm...]
where the time goes in v3:
time: 165 us
  Pallas kernels  164 us (99%)
    pallas_call x1, Pallas kernels, on_device(): pl.pallas_call(kernel, out_shape=(rows, rows), in_specs=[vmem] * 7 + [hbm...  162 us

profile of v3, /device:TPU:38, one launch (start us, length us, event | category | flops | bytes accessed | tf_op | source)
XLA Modules:
  0.0 164.7 jit_solution(2328799344273745004)
XLA Ops:
  0.6 162.0 %relay_experts.1 = (bf16[64,3584]{1,0:T(8,128)(2,1)}, bf16[64,3584]{1,0:T(8,128)(2,1)}) custom-call(bf16[64,3584]{1,0:T(8,128)(2,1)} %bitcast.11, bf16[64,3584]{1,0:T(8,128)(2,1)} %bitcast.12, bf16[64,3584]{1,0:T(8,128)(2,1)} %bitcast.13, s32[1,1024]{1,0:T(1,128)} %ids_f.1, bf16[1,1024]{1,0:T(2,128)(2,1)} %probs_f.1, s32[1,1024]{1,0:T(1,128)} %ids_b.1, ...), custom_call_target="tpu_custom_call" | custom-call | flops 7049999872 | bytes 12000000 | tf_op jit(solution)/shard_map/relay_experts/pallas_call | solution.py:848
  162.6 2.1 %give.1 = (bf16[64,3584]{1,0:T(8,128)(2,1)}, bf16[64,3584]{1,0:T(8,128)(2,1)}) custom-call(bf16[64,3584]{1,0:T(8,128)(2,1)} %get-tuple-element.6.from_f, bf16[64,3584]{1,0:T(8,128)(2,1)} %get-tuple-element.7.from_b), custom_call_target="tpu_custom_call" | custom-call | tf_op jit(solution)/shard_map/give/pallas_call | solution.py:904

commit v4 on v3

--- a/solution.py
+++ b/solution.py
@@ -13,6 +13,7 @@
 D = 3584
 HID = 384
 TOK = 64
+TOKENS = 1024
 ROWS = 2 * SLOT
 HALF = D // 2
 WIDE = 256
@@ -24,9 +25,9 @@
 RECV, HOME, TRANSIT = 8, 17, 18
 S_A, G_A, S_B, G_B, X_B, X_A = range(6)
 R_A, R_B, F_B, F_A = range(4)
-PARTS = (2, 2, 2, 2)
+PARTS = (1, 1, 2, 2)
 DEPTH = 3
-RAWS = (0, 1, 2)
+RAWS = (0, 1)
 TENSOR = (0, 1, 0, 1, 2, 2)
 
 ORDER = (
@@ -34,12 +35,15 @@
         (),
         (),
         ((0, 0, 0), (0, 1, 0)),
-        ((0, 0, 1), (2, 0, 0), (2, 1, 0)),
+        ((0, 0, 1), (2, 0, 0)),
         (),
         ((1, 0, 0), (1, 1, 0)),
-        ((0, 1, 1), (2, 0, 1), (3, 0, 0), (1, 0, 1), (3, 1, 0)),
-        ((0, 0, 2), (5, 1, 0), (3, 0, 1)),
-        ((1, 1, 1), (2, 1, 1), (5, 0, 0), (4, 0, 0), (4, 1, 0), (1, 0, 2), (2, 0, 2), (3, 1, 1), (4, 0, 1), (3, 0, 2), (5, 0, 1)),
+        ((2, 1, 0), (0, 1, 1), (3, 0, 0), (1, 0, 1), (3, 1, 0), (2, 0, 1), (0, 0, 2)),
+        ((1, 1, 1), (2, 1, 1), (3, 0, 1)),
+        ((5, 0, 0), (5, 1, 0), (1, 0, 2), (3, 1, 1), (2, 0, 2), (4, 0, 0), (4, 1, 0), (3, 0, 2), (4, 0, 1), (5, 0, 1)),
+        (),
+        (),
+        (),
         (),
         (),
         (),
@@ -49,60 +53,56 @@
         (),
         (),
         ((6, 1, 0), (6, 1, 1)),
-        (),
-        (),
-        (),
-        ((7, 1, 0), (5, 1, 1), (7, 1, 1)),
-        ((6, 1, 2), (7, 1, 2), (5, 0, 2), (6, 1, 3), (4, 1, 1), (7, 1, 3), (6, 1, 4), (4, 0, 2)),
-        (),
-        ((7, 1, 4),),
-        (),
-        (),
-        (),
-        (),
-        (),
-        ((8, 1, 0),),
-        ((8, 1, 1),),
-        (),
-        ((9, 1, 0), (9, 1, 1), (8, 1, 2), (6, 0, 3), (9, 1, 2), (7, 0, 3), (8, 1, 3), (9, 1, 3)),
-        (),
-        ((8, 1, 4),),
-        ((8, 0, 3), (9, 1, 4)),
-        (),
-        ((8, 0, 4),),
-        (),
-        ((10, 1, 0),),
-        (),
-        ((9, 0, 3),),
-        ((11, 1, 0), (9, 0, 4), (8, 1, 5), (10, 1, 1)),
-        ((9, 1, 5), (11, 1, 1), (10, 1, 2), (11, 1, 2), (10, 1, 3), (11, 1, 3), (6, 1, 5), (7, 1, 5)),
-        (),
-        ((10, 1, 4),),
-        ((6, 0, 4), (11, 1, 4)),
-        ((7, 0, 4),),
+        ((6, 1, 2), (4, 1, 1), (6, 1, 3)),
+        ((6, 1, 4),),
+        (),
+        (),
+        (),
+        ((4, 0, 2),),
+        (),
+        (),
+        (),
+        (),
+        (),
+        ((8, 1, 0), (8, 1, 1), (8, 1, 2), (5, 1, 1), (8, 1, 3), (8, 1, 4), (5, 0, 2)),
+        (),
+        (),
+        (),
+        (),
+        (),
+        ((8, 0, 3),),
+        ((10, 1, 0), (10, 1, 1)),
+        (),
+        (),
+        ((8, 0, 4), (11, 1, 0), (11, 1, 1), (8, 1, 5), (10, 1, 2)),
+        ((11, 1, 2), (10, 1, 3), (11, 1, 3), (10, 0, 3), (11, 0, 3), (10, 1, 4), (11, 1, 4)),
+        ((10, 1, 5),),
+        ((11, 1, 5), (10, 0, 4)),
+        (),
+        (),
         (),
         (),
         ((12, 1, 0),),
-        (),
-        ((10, 0, 3),),
-        ((13, 1, 0), (11, 0, 3), (12, 1, 1), (13, 1, 1), (10, 1, 5), (10, 0, 4), (11, 1, 5), (11, 0, 4), (12, 1, 2), (13, 1, 2)),
-        (),
-        ((12, 0, 3), (12, 1, 3), (13, 1, 3)),
-        ((13, 0, 3), (12, 0, 4), (12, 1, 4), (13, 1, 4), (13, 0, 4), (12, 1, 5)),
-        ((13, 1, 5),),
+        ((12, 1, 1),),
+        ((6, 0, 3),),
+        ((11, 0, 4), (13, 1, 0), (13, 1, 1), (12, 1, 2), (6, 1, 5), (6, 0, 4)),
+        ((13, 1, 2),),
+        ((12, 1, 3),),
+        ((12, 0, 3), (13, 1, 3), (13, 0, 3), (12, 1, 4), (13, 1, 4), (12, 0, 4)),
+        ((13, 0, 4), (12, 1, 5), (13, 1, 5)),
         (),
     ),
     (
         (),
         ((14, 1, 0),),
         ((0, 0, 0),),
-        ((0, 0, 1), (0, 1, 2), (2, 0, 0), (0, 0, 2)),
-        (),
-        ((15, 1, 0), (1, 0, 0)),
-        ((0, 1, 3), (2, 0, 1), (1, 0, 1)),
-        ((2, 0, 2),),
-        ((0, 1, 4), (3, 0, 0), (1, 1, 2), (1, 0, 2), (1, 1, 3), (0, 0, 3), (16, 1, 0), (3, 0, 1), (1, 1, 4), (3, 0, 2)),
-        ((4, 0, 0), (1, 0, 3), (2, 0, 3), (0, 1, 5), (4, 0, 1), (2, 1, 2)),
+        ((0, 0, 1), (0, 1, 2), (2, 0, 0)),
+        (),
+        ((1, 0, 0), (15, 1, 0)),
+        (),
+        ((0, 1, 3), (0, 0, 2), (2, 0, 1), (1, 0, 1)),
+        ((3, 0, 0), (1, 1, 2), (1, 0, 2), (2, 1, 2), (2, 0, 2), (1, 1, 3), (0, 0, 3), (2, 1, 3), (3, 0, 1), (1, 1, 4), (3, 0, 2), (2, 1, 4)),
+        ((1, 0, 3), (0, 1, 4), (2, 0, 3), (0, 1, 5), (4, 0, 0), (3, 1, 2)),
         (),
         (),
         ((1, 1, 5), (3, 0, 3)),
@@ -110,122 +110,123 @@
         (),
         (),
         (),
-        ((4, 0, 2),),
-        ((2, 1, 3),),
-        (),
-        (),
-        (),
-        ((5, 0, 0), (2, 1, 4)),
-        (),
-        (),
-        ((2, 1, 5), (5, 0, 1)),
-        (),
-        (),
-        (),
-        (),
-        ((5, 0, 2),),
-        ((3, 1, 2),),
-        (),
-        ((3, 1, 3), (6, 1, 1), (6, 1, 2), (3, 1, 4), (7, 1, 1), (3, 1, 5), (7, 1, 2), (6, 1, 3), (7, 1, 3), (4, 1, 2), (5, 0, 3), (4, 1, 3), (6, 1, 4), (7, 1, 4), (4, 1, 4), (6, 0, 2), (4, 0, 3), (7, 0, 2), (8, 1, 1)),
+        ((4, 0, 1), (2, 1, 5)),
+        (),
+        (),
+        (),
+        ((4, 0, 2), (3, 1, 3)),
+        (),
+        (),
+        ((3, 1, 4), (5, 0, 0)),
+        (),
+        (),
+        (),
+        (),
+        ((5, 0, 1), (4, 1, 0)),
+        (),
+        (),
+        ((5, 0, 2), (3, 1, 5), (6, 1, 1), (4, 1, 1), (6, 1, 2), (4, 1, 2), (6, 1, 3), (4, 1, 3), (6, 1, 4), (4, 1, 4), (5, 1, 0), (4, 0, 3), (5, 1, 1), (8, 1, 1), (5, 1, 2)),
+        (),
+        (),
         ((4, 1, 5), (8, 1, 2)),
-        ((9, 1, 1), (8, 0, 2)),
-        ((9, 1, 2),),
-        (),
-        (),
-        ((8, 0, 3), (8, 1, 3)),
-        (),
-        (),
-        ((9, 1, 3), (9, 0, 2)),
-        ((8, 1, 4), (9, 0, 3), (9, 1, 4), (8, 0, 4), (9, 0, 4), (5, 1, 2), (5, 1, 3), (10, 1, 1), (11, 1, 1), (5, 1, 4), (10, 1, 2), (5, 1, 5)),
-        (),
-        ((11, 1, 2),),
-        (),
-        ((6, 0, 3), (10, 1, 3)),
-        (),
-        ((11, 1, 3),),
-        (),
-        (),
-        (),
-        (),
-        ((7, 0, 3), (10, 1, 4), (11, 1, 4), (10, 0, 2), (11, 0, 2), (6, 0, 4), (7, 0, 4), (10, 0, 3), (11, 0, 3), (12, 1, 1), (13, 1, 1), (10, 0, 4), (11, 0, 4), (12, 1, 2), (13, 1, 2), (12, 0, 2), (13, 0, 2)),
-        ((12, 0, 3),),
-        ((12, 1, 3), (13, 0, 3)),
-        ((13, 1, 3), (12, 1, 4), (12, 0, 4), (13, 1, 4), (13, 0, 4)),
-        (),
+        (),
+        (),
+        (),
+        (),
+        (),
+        ((8, 1, 3), (8, 0, 2)),
+        ((8, 1, 4), (8, 0, 3), (8, 0, 4), (5, 0, 3), (5, 1, 3), (10, 1, 1), (5, 1, 4), (10, 1, 2), (11, 1, 1), (10, 0, 2), (11, 1, 2), (11, 0, 2)),
+        (),
+        (),
+        ((5, 1, 5), (10, 1, 3)),
+        ((10, 0, 3), (11, 1, 3)),
+        (),
+        (),
+        (),
+        ((10, 1, 4),),
+        (),
+        ((6, 0, 2), (11, 1, 4)),
+        ((11, 0, 3), (10, 0, 4), (6, 0, 3)),
+        (),
+        ((11, 0, 4), (12, 1, 1), (12, 1, 2), (6, 0, 4), (13, 1, 1), (12, 0, 2), (13, 1, 2), (12, 1, 3), (13, 0, 2), (12, 0, 3)),
+        ((13, 0, 3), (13, 1, 3)),
+        ((12, 0, 4), (12, 1, 4), (13, 1, 4), (13, 0, 4)),
         (),
     ),
     (
         (),
         ((14, 0, 0),),
         ((0, 1, 0),),
-        ((0, 1, 1), (0, 0, 2), (2, 1, 0), (0, 1, 2)),
-        (),
-        ((15, 0, 0), (1, 1, 0)),
-        ((0, 0, 3), (2, 1, 1), (1, 1, 1)),
-        ((2, 1, 2),),
-        ((0, 0, 4), (3, 1, 0), (1, 0, 2), (1, 1, 2), (1, 0, 3), (0, 1, 3), (16, 0, 0), (3, 1, 1), (1, 0, 4), (3, 1, 2)),
-        ((4, 1, 0), (1, 1, 3), (2, 1, 3), (0, 0, 5), (4, 1, 1), (2, 0, 2)),
-        (),
-        (),
-        ((3, 1, 3), (1, 0, 5)),
-        (),
-        (),
-        (),
-        (),
-        ((4, 1, 2),),
-        ((2, 0, 3),),
-        (),
-        (),
-        (),
-        ((5, 1, 0), (2, 0, 4)),
-        (),
-        (),
-        ((5, 1, 1), (2, 0, 5)),
-        (),
-        (),
-        (),
-        (),
-        ((5, 1, 2),),
-        ((3, 0, 2),),
-        (),
-        ((3, 0, 3), (6, 0, 1), (6, 0, 2), (3, 0, 4), (7, 0, 1), (3, 0, 5), (7, 0, 2), (6, 0, 3), (7, 0, 3), (4, 0, 2), (5, 1, 3), (4, 0, 3), (6, 0, 4), (7, 0, 4), (4, 0, 4), (6, 1, 2), (4, 1, 3), (7, 1, 2), (8, 0, 1)),
+        ((0, 1, 1), (0, 0, 2), (2, 1, 0)),
+        (),
+        ((1, 1, 0), (15, 0, 0)),
+        (),
+        ((0, 0, 3), (0, 1, 2), (2, 1, 1), (1, 1, 1)),
+        ((3, 1, 0), (1, 0, 2), (1, 1, 2), (2, 0, 2), (2, 1, 2), (1, 0, 3), (0, 1, 3), (2, 0, 3), (3, 1, 1), (1, 0, 4), (3, 1, 2), (2, 0, 4)),
+        ((1, 1, 3), (0, 0, 4), (2, 1, 3), (0, 0, 5), (4, 1, 0), (3, 0, 2)),
+        (),
+        (),
+        ((1, 0, 5), (3, 1, 3)),
+        (),
+        (),
+        (),
+        (),
+        ((4, 1, 1),),
+        ((2, 0, 5),),
+        (),
+        (),
+        ((4, 1, 2), (3, 0, 3)),
+        (),
+        (),
+        ((3, 0, 4), (5, 1, 0)),
+        (),
+        (),
+        (),
+        (),
+        ((5, 1, 1),),
+        ((4, 0, 0),),
+        (),
+        ((5, 1, 2), (3, 0, 5), (6, 0, 1), (4, 0, 1), (6, 0, 2), (4, 0, 2), (6, 0, 3), (4, 0, 3), (6, 0, 4), (4, 0, 4), (5, 0, 0), (4, 1, 3), (5, 0, 1), (8, 0, 1), (5, 0, 2)),
+        (),
+        (),
         ((4, 0, 5), (8, 0, 2)),
-        ((9, 0, 1), (8, 1, 2)),
-        ((9, 0, 2),),
-        (),
-        (),
-        ((8, 1, 3), (8, 0, 3)),
-        (),
-        (),
-        ((9, 0, 3), (9, 1, 2)),
-        ((8, 0, 4), (9, 1, 3), (9, 0, 4), (8, 1, 4), (9, 1, 4), (5, 0, 2), (5, 0, 3), (10, 0, 1), (11, 0, 1), (5, 0, 4), (10, 0, 2), (5, 0, 5)),
-        (),
-        ((11, 0, 2),),
-        (),
-        ((6, 1, 3), (10, 0, 3)),
-        (),
-        ((11, 0, 3),),
-        (),
-        (),
-        (),
-        (),
-        ((7, 1, 3), (10, 0, 4), (11, 0, 4), (10, 1, 2), (11, 1, 2), (6, 1, 4), (7, 1, 4), (10, 1, 3), (11, 1, 3), (12, 0, 1), (13, 0, 1), (10, 1, 4), (11, 1, 4), (12, 0, 2), (13, 0, 2), (12, 1, 2), (13, 1, 2)),
-        ((12, 1, 3),),
-        ((12, 0, 3), (13, 1, 3)),
-        ((13, 0, 3), (12, 0, 4), (12, 1, 4), (13, 0, 4), (13, 1, 4)),
-        (),
+        (),
+        (),
+        (),
+        (),
+        (),
+        ((8, 0, 3), (8, 1, 2)),
+        ((8, 0, 4), (8, 1, 3), (8, 1, 4), (5, 1, 3), (5, 0, 3), (10, 0, 1), (5, 0, 4), (10, 0, 2), (11, 0, 1), (10, 1, 2), (11, 0, 2), (11, 1, 2)),
+        (),
+        (),
+        ((5, 0, 5), (10, 0, 3)),
+        ((10, 1, 3), (11, 0, 3)),
+        (),
+        (),
+        (),
+        ((10, 0, 4),),
+        (),
+        ((6, 1, 2), (11, 0, 4)),
+        ((11, 1, 3), (10, 1, 4), (6, 1, 3)),
+        (),
+        ((11, 1, 4), (12, 0, 1), (12, 0, 2), (6, 1, 4), (13, 0, 1), (12, 1, 2), (13, 0, 2), (12, 0, 3), (13, 1, 2), (12, 1, 3)),
+        ((13, 0, 3), (13, 1, 3)),
+        ((12, 0, 4), (12, 1, 4), (13, 0, 4), (13, 1, 4)),
         (),
     ),
     (
         (),
         (),
         ((0, 0, 0), (0, 1, 0)),
-        ((0, 1, 1), (2, 1, 0), (2, 0, 0)),
+        ((0, 1, 1), (2, 1, 0)),
         (),
         ((1, 0, 0), (1, 1, 0)),
-        ((0, 0, 1), (2, 1, 1), (3, 1, 0), (1, 1, 1), (3, 0, 0)),
-        ((0, 1, 2), (5, 0, 0), (3, 1, 1)),
-        ((1, 0, 1), (2, 0, 1), (5, 1, 0), (4, 1, 0), (4, 0, 0), (1, 1, 2), (2, 1, 2), (3, 0, 1), (4, 1, 1), (3, 1, 2), (5, 1, 1)),
+        ((2, 0, 0), (0, 0, 1), (3, 1, 0), (1, 1, 1), (3, 0, 0), (2, 1, 1), (0, 1, 2)),
+        ((1, 0, 1), (2, 0, 1)),
+        ((3, 1, 1), (5, 1, 0), (5, 0, 0), (1, 1, 2), (3, 0, 1), (2, 1, 2), (4, 1, 0), (4, 0, 0), (3, 1, 2), (4, 1, 1), (5, 1, 1)),
+        (),
+        (),
+        (),
         (),
         (),
         (),
@@ -235,47 +236,43 @@
         (),
         (),
         ((6, 0, 0), (6, 0, 1)),
-        (),
-        (),
-        (),
-        ((7, 0, 0), (5, 0, 1), (7, 0, 1)),
-        ((6, 0, 2), (7, 0, 2), (5, 1, 2), (6, 0, 3), (4, 0, 1), (7, 0, 3), (6, 0, 4), (4, 1, 2)),
-        (),
-        ((7, 0, 4),),
-        (),
-        (),
-        (),
-        (),
-        (),
-        ((8, 0, 0),),
-        ((8, 0, 1),),
-        (),
-        ((9, 0, 0), (9, 0, 1), (8, 0, 2), (6, 1, 3), (9, 0, 2), (7, 1, 3), (8, 0, 3), (9, 0, 3)),
-        (),
-        ((8, 0, 4),),
-        ((8, 1, 3), (9, 0, 4)),
-        (),
-        ((8, 1, 4),),
-        (),
-        ((10, 0, 0),),
-        (),
-        ((9, 1, 3),),
-        ((11, 0, 0), (9, 1, 4), (8, 0, 5), (10, 0, 1)),
-        ((9, 0, 5), (11, 0, 1), (10, 0, 2), (11, 0, 2), (10, 0, 3), (11, 0, 3), (6, 0, 5), (7, 0, 5)),
-        (),
-        ((10, 0, 4),),
-        ((6, 1, 4), (11, 0, 4)),
-        ((7, 1, 4),),
+        ((6, 0, 2), (4, 0, 1), (6, 0, 3)),
+        ((6, 0, 4),),
+        (),
+        (),
+        (),
+        ((4, 1, 2),),
+        (),
+        (),
+        (),
+        (),
+        (),
+        ((8, 0, 0), (8, 0, 1), (8, 0, 2), (5, 0, 1), (8, 0, 3), (8, 0, 4), (5, 1, 2)),
+        (),
+        (),
+        (),
+        (),
+        (),
+        ((8, 1, 3),),
+        ((10, 0, 0), (10, 0, 1)),
+        (),
+        (),
+        ((8, 1, 4), (11, 0, 0), (11, 0, 1), (8, 0, 5), (10, 0, 2)),
+        ((11, 0, 2), (10, 0, 3), (11, 0, 3), (10, 1, 3), (11, 1, 3), (10, 0, 4), (11, 0, 4)),
+        ((10, 0, 5),),
+        ((11, 0, 5), (10, 1, 4)),
+        (),
+        (),
         (),
         (),
         ((12, 0, 0),),
-        (),
-        ((10, 1, 3),),
-        ((13, 0, 0), (11, 1, 3), (12, 0, 1), (13, 0, 1), (10, 0, 5), (10, 1, 4), (11, 0, 5), (11, 1, 4), (12, 0, 2), (13, 0, 2)),
-        (),
-        ((12, 0, 3), (12, 1, 3), (13, 0, 3)),
-        ((13, 1, 3), (12, 0, 4), (12, 1, 4), (13, 0, 4), (13, 1, 4), (12, 0, 5)),
-        ((13, 0, 5),),
+        ((12, 0, 1),),
+        ((6, 1, 3),),
+        ((11, 1, 4), (13, 0, 0), (13, 0, 1), (12, 0, 2), (6, 0, 5), (6, 1, 4)),
+        ((13, 0, 2),),
+        ((12, 0, 3),),
+        ((12, 1, 3), (13, 0, 3), (13, 1, 3), (12, 0, 4), (13, 0, 4), (12, 1, 4)),
+        ((13, 1, 4), (12, 0, 5), (13, 0, 5)),
         (),
     ),
 )
@@ -326,15 +323,21 @@
     held_fwd,
     held_grad,
     saved,
-    ids_f,
-    probs_f,
-    ids_b,
-    probs_b,
+    ids_f_hbm,
+    probs_f_hbm,
+    ids_b_hbm,
+    probs_b_hbm,
     w_gate_hbm,
     w_up_hbm,
     w_down_hbm,
     out_f,
     out_b,
+    saved_rows,
+    ids_f,
+    probs_f,
+    ids_b,
+    probs_b,
+    result,
     w_gate,
     w_up,
     w_down,
@@ -353,6 +356,8 @@
     gathering,
     scattering,
     w_sem,
+    in_sem,
+    out_sem,
     shift_send,
     shift_recv,
     y_send_sem,
@@ -382,6 +387,20 @@
     for device in (right, left, across, after, before):
         pl.semaphore_signal(barrier, inc=1, device_id=device, device_id_type=MESH)
 
+    input_copies = [
+        pltpu.make_async_copy(src, dst, in_sem.at[n])
+        for n, (src, dst) in enumerate(
+            (
+                (ids_b_hbm, ids_b),
+                (probs_b_hbm, probs_b),
+                (saved, saved_rows),
+                (ids_f_hbm, ids_f),
+                (probs_f_hbm, probs_f),
+            )
+        )
+    ]
+    for copy in input_copies:
+        copy.start()
     weight_copies = [
         pltpu.make_async_copy(w_gate_hbm, w_gate, w_sem.at[0]),
         pltpu.make_async_copy(w_up_hbm, w_up, w_sem.at[1]),
@@ -433,7 +452,7 @@
         rank_col = jnp.sum(jnp.where((row == col) & (j < i), one, none), axis=1, keepdims=True)
         return row * SLOT + rank_row, col * SLOT + rank_col, upright(part_of(probs_ref, position))
 
-    sources = (saved, g_rows, x_rows)
+    sources = (saved_rows, g_rows, x_rows)
 
     def choose(rows, slot_row, blocks):
         experts = [2 * side + line for side in (plane, 1 - plane) for line in (half, 1 - half)]
@@ -478,8 +497,9 @@
         )
 
     def raw_copy(t, way):
+        rows = saved if t == 0 else sources[t]
         return remote(
-            sources[t], raw.at[t], raw_send_sem.at[t], raw_recv_sem.at[t], right if way == 0 else left
+            rows, raw.at[t], raw_send_sem.at[t], raw_recv_sem.at[t], right if way == 0 else left
         )
 
     def y_copy(t, n):
@@ -702,12 +722,23 @@
         blocks = (y_back.at[t, 0], y_back.at[t, 1])
         combine(t, slot_cols[t], 1 - plane, blocks, (g_rows, x_rows)[t], total.at[t], STARTS)
 
+    def output_copies(t, p=None):
+        ends = (0, HALF) if p is None or PARTS[F_A] == 1 else ((0, 4 * WIDE), (4 * WIDE, HALF))[p]
+        return [
+            pltpu.make_async_copy(
+                result.at[t, :, pl.ds(side + ends[0], ends[1] - ends[0])],
+                (out_b, out_f)[t].at[:, pl.ds(side + ends[0], ends[1] - ends[0])],
+                out_sem.at[t, p or 0, n],
+            )
+            for n, side in enumerate((0, HALF))
+        ]
+
     def combine_a(t, p=None):
         side = (R_A, F_A)[t]
         join_home(side, pl.ds(0, HALF) if p is None else columns(side, p))
         starts = STARTS if p is None or PARTS[side] == 1 else (STARTS[:4], STARTS[4:])[p]
         blocks = (ret.at[side, q + 2], ret.at[side, HOME])
-        combine(t, slot_cols[t], plane, blocks, total.at[t], (out_b, out_f)[t], starts)
+        combine(t, slot_cols[t], plane, blocks, total.at[t], result.at[t], starts)
 
     shift_g = remote(held_grad, g_rows, shift_send.at[0], shift_recv.at[0], before)
     shift_x = remote(held_fwd, x_rows, shift_send.at[1], shift_recv.at[1], after)
@@ -737,12 +768,15 @@
                 edge_copy(t, n).start()
 
     piece()
+    pl.semaphore_wait(barrier, 5)
+    shift_g.start()
+
+    piece()
+    for copy in input_copies:
+        copy.wait()
     slot_row_b, slot_col_b, prob_b = routing(ids_b, probs_b, position)
     choose_own(0, slot_row_b)
-    pl.semaphore_wait(barrier, 5)
-    shift_g.start()
-
-    piece()
+
     piece()
     slot_row_f, slot_col_f, prob_f = routing(ids_f, probs_f, position)
     neighbour = position + jnp.where(q == 0, 1, 0) - jnp.where(q == 3, 1, 0)
@@ -767,12 +801,12 @@
     cross(1)
     shift_x.start()
     pick_near(0)
+    pick_near(1)
 
     piece()
     shift_x.wait_recv()
     choose_own(2, slot_row_f)
     cross(2)
-    pick_near(1)
 
     for saved_side, grad_side, back in ((S_A, G_A, R_A), (S_B, G_B, R_B)):
         piece(all_of(saved_side))
@@ -809,11 +843,15 @@
     combine_b(0)
     piece(home_of(R_A, range(PARTS[R_A])))
     combine_a(0)
+    for copy in output_copies(0):
+        copy.start()
     piece()
     combine_b(1)
     for p in range(PARTS[F_A]):
         piece(home_of(F_A, (p,)))
         combine_a(1, p)
+        for copy in output_copies(1, p):
+            copy.start()
 
     shift_g.wait_send()
     shift_x.wait_send()
@@ -833,6 +871,12 @@
                 for op in link[-DEPTH:]:
                     described(place, op).wait_send()
 
+    for copy in output_copies(0):
+        copy.wait()
+    for p in range(PARTS[F_A]):
+        for copy in output_copies(1, p):
+            copy.wait()
+
 
 def give(from_f, from_b, to_f, to_b):
     to_f[...] = from_f[...]
@@ -848,9 +892,15 @@
     fwd, grad = pl.pallas_call(
         kernel,
         out_shape=(rows, rows),
-        in_specs=[vmem] * 7 + [hbm] * 3,
-        out_specs=(vmem, vmem),
+        in_specs=[hbm] * 10,
+        out_specs=(hbm, hbm),
         scratch_shapes=[
+            pltpu.VMEM((TOK, D), BF16),
+            pltpu.VMEM((1, TOKENS), jnp.int32),
+            pltpu.VMEM((1, TOKENS), BF16),
+            pltpu.VMEM((1, TOKENS), jnp.int32),
+            pltpu.VMEM((1, TOKENS), BF16),
+            pltpu.VMEM((2, TOK, D), BF16),
             pltpu.VMEM((D, HID), BF16),
             pltpu.VMEM((D, HID), BF16),
             pltpu.VMEM((HID, D), BF16),
@@ -869,6 +919,8 @@
             pltpu.VMEM((2 * ALL, 2 * ALL), BF16),
             pltpu.VMEM((2 * ALL, 2 * ALL), BF16),
             pltpu.SemaphoreType.DMA((3,)),
+            pltpu.SemaphoreType.DMA((5,)),
+            pltpu.SemaphoreType.DMA((2, 2, 2)),
             pltpu.SemaphoreType.DMA((2,)),
             pltpu.SemaphoreType.DMA((2,)),
             pltpu.SemaphoreType.DMA((5, 2)),

time: 165 us -> 163 us (0.988)
  Pallas kernels: 164 us -> 162 us
    pallas_call x1, Pallas kernels: 162 us -> 160 us  [on_device(): pl.pallas_call(kernel, out_shape=(rows, rows), in_specs=[hbm] * 10, out_s...]
where the time goes in v4:
time: 163 us
  Pallas kernels  162 us (99%)
    pallas_call x1, Pallas kernels, on_device(): pl.pallas_call(kernel, out_shape=(rows, rows), in_specs=[hbm] * 10, out_s...  160 us

profile of v4, /device:TPU:38, one launch (start us, length us, event | category | flops | bytes accessed | tf_op | source)
XLA Modules:
  0.0 162.9 jit_solution(13512089737317911557)
XLA Ops:
  0.6 160.1 %relay_experts.1 = (bf16[64,3584]{1,0:T(8,128)(2,1)}, bf16[64,3584]{1,0:T(8,128)(2,1)}) custom-call(bf16[64,3584]{1,0:T(8,128)(2,1)} %bitcast.11, bf16[64,3584]{1,0:T(8,128)(2,1)} %bitcast.12, bf16[64,3584]{1,0:T(8,128)(2,1)} %bitcast.13, s32[1,1024]{1,0:T(1,128)} %ids_f_hbm.1, bf16[1,1024]{1,0:T(2,128)(2,1)} %probs_f_hbm.1, s32[1,1024]{1,0:T(1,128)} %ids_b_hbm.1, ...), custom_call_target="tpu_custom_call" | custom-call | flops 7049999872 | bytes 12000000 | tf_op jit(solution)/shard_map/relay_experts/pallas_call | solution.py:892
  160.7 2.1 %give.1 = (bf16[64,3584]{1,0:T(8,128)(2,1)}, bf16[64,3584]{1,0:T(8,128)(2,1)}) custom-call(bf16[64,3584]{1,0:T(8,128)(2,1)} %get-tuple-element.6.from_f, bf16[64,3584]{1,0:T(8,128)(2,1)} %get-tuple-element.7.from_b), custom_call_target="tpu_custom_call" | custom-call | tf_op jit(solution)/shard_map/give/pallas_call | solution.py:956

commit v5 on v4

--- a/solution.py
+++ b/solution.py
@@ -406,8 +406,6 @@
         pltpu.make_async_copy(w_up_hbm, w_up, w_sem.at[1]),
         pltpu.make_async_copy(w_down_hbm, w_down, w_sem.at[2]),
     ]
-    for copy in weight_copies:
-        copy.start()
 
     def remote(src, dst, send_sem, recv_sem, device):
         return pltpu.make_async_remote_copy(
@@ -774,6 +772,8 @@
     piece()
     for copy in input_copies:
         copy.wait()
+    for copy in weight_copies:
+        copy.start()
     slot_row_b, slot_col_b, prob_b = routing(ids_b, probs_b, position)
     choose_own(0, slot_row_b)
 
@@ -878,15 +878,23 @@
             copy.wait()
 
 
-def give(from_f, from_b, to_f, to_b):
-    to_f[...] = from_f[...]
-    to_b[...] = from_b[...]
+def give(from_f, from_b, to_f, to_b, held, load_sem, store_sem):
+    loads, stores = [], []
+    for n, (source, target) in enumerate(((from_f, to_f), (from_b, to_b))):
+        loads.append(pltpu.make_async_copy(source, held.at[n], load_sem.at[n]))
+        stores.append(pltpu.make_async_copy(held.at[n], target, store_sem.at[n]))
+    for load in loads:
+        load.start()
+    for load, store in zip(loads, stores):
+        load.wait()
+        store.start()
+    for store in stores:
+        store.wait()
 
 
 def on_device(
     held_fwd, ids_fwd, probs_fwd, saved_in, held_grad, ids_bwd, probs_bwd, w_gate, w_up, w_down
 ):
-    vmem = pl.BlockSpec(memory_space=pltpu.VMEM)
     hbm = pl.BlockSpec(memory_space=pl.ANY)
     rows = jax.ShapeDtypeStruct((TOK, D), BF16)
     fwd, grad = pl.pallas_call(
@@ -956,8 +964,13 @@
     fwd, grad = pl.pallas_call(
         give,
         out_shape=(rows, rows),
-        in_specs=[vmem, vmem],
-        out_specs=(vmem, vmem),
+        in_specs=[hbm, hbm],
+        out_specs=(hbm, hbm),
+        scratch_shapes=[
+            pltpu.VMEM((2, TOK, D), BF16),
+            pltpu.SemaphoreType.DMA((2,)),
+            pltpu.SemaphoreType.DMA((2,)),
+        ],
         name="give",
     )(fwd, grad)
     return (fwd[None], grad[None])

time: 163 us -> 163 us (level)
  no operation moved by 1% of the time
where the time goes in v5:
time: 163 us
  Pallas kernels  162 us (99%)
    pallas_call x1, Pallas kernels, on_device(): pl.pallas_call(kernel, out_shape=(rows, rows), in_specs=[hbm] * 10, out_s...  160 us

profile of v5, /device:TPU:38, one launch (start us, length us, event | category | flops | bytes accessed | tf_op | source)
XLA Modules:
  0.0 162.7 jit_solution(1941721564587601539)
XLA Ops:
  0.6 159.9 %relay_experts.1 = (bf16[64,3584]{1,0:T(8,128)(2,1)}, bf16[64,3584]{1,0:T(8,128)(2,1)}) custom-call(bf16[64,3584]{1,0:T(8,128)(2,1)} %bitcast.11, bf16[64,3584]{1,0:T(8,128)(2,1)} %bitcast.12, bf16[64,3584]{1,0:T(8,128)(2,1)} %bitcast.13, s32[1,1024]{1,0:T(1,128)} %ids_f_hbm.1, bf16[1,1024]{1,0:T(2,128)(2,1)} %probs_f_hbm.1, s32[1,1024]{1,0:T(1,128)} %ids_b_hbm.1, ...), custom_call_target="tpu_custom_call" | custom-call | flops 7049999872 | bytes 12000000 | tf_op jit(solution)/shard_map/relay_experts/pallas_call | solution.py:900
  160.5 2.0 %give.1 = (bf16[64,3584]{1,0:T(8,128)(2,1)}, bf16[64,3584]{1,0:T(8,128)(2,1)}) custom-call(bf16[64,3584]{1,0:T(8,128)(2,1)} %get-tuple-element.6.from_f, bf16[64,3584]{1,0:T(8,128)(2,1)} %get-tuple-element.7.from_b), custom_call_target="tpu_custom_call" | custom-call | tf_op jit(solution)/shard_map/give/pallas_call | solution.py:964
